TPU v7x, 512 devices: a whole 4x8x8 slice. The times are simulated.
512 devices in a mesh: seq: 128 (over z, y, core), head: 4 (over x).
Axes of the slice: x: 4, y: 8, z: 8, core: 2. Of those that a mesh axis runs over, the one named last changes fastest.
Arguments:
- queries: bfloat16 [65536, 4096], P(('seq', 'head'))
- image_keys: bfloat16 [512, 512, 512], P('seq', None, 'head')
- image_values: bfloat16 [512, 512, 512], P('seq', None, 'head'), may hold values from -6 to 6
- out_grad: bfloat16 [65536, 4096], P(('seq', 'head')), may hold values from -6 to 6
- tile_counts: int32 [512], replicated, may hold values from 1 to 4, as said below
- block_reads: int32 [128, 2], replicated, may hold values from 0 to 511, as said below
Outputs:
- query_grad: bfloat16 [65536, 4096], P(('seq', 'head'))
- key_grad: bfloat16 [512, 512, 512], P('seq', None, 'head')
- value_grad: bfloat16 [512, 512, 512], P('seq', None, 'head')
Inputs may be any that keep to these rules, and one draw needn't show every extreme that they name: `block_reads`: image i is owned by index i // 4 of seq. The 2 images read by the blocks of one index d of seq are all different, and each is owned by an index within 2 of d, cyclically (possibly d itself). No owner owns more than 1 of these 2 images, and some owner owns exactly 1 of them. `tile_counts`: some image has 4 tiles.
All inputs are finite; a program needn't handle non-finite values.
Results may differ from a plain program's by a relative error of at most 0.012.
The roundings to bfloat16 on the way count: a program that leaves them out, or rounds other values in their place, can miss the bound.
Values may be sent and summed in bfloat16 or wider, within the bound.
A program may use at most 64 MiB of HBM per device.

v0:
```python
import jax
import jax.numpy as jnp
from jax import lax
from jax.sharding import PartitionSpec as P

HDIM = 128
TILE_TOK = 128
READS = 2
SPAN = 2
BLK = 512


def passed_along(block, axis, distance):
    devices = range(lax.axis_size(axis))
    route = [((i - distance) % len(devices), i) for i in devices]
    return lax.ppermute(block, axis, route)


def slot_tables(need_rows, owner_id, per_owner, capacity):
    owned = need_rows // per_owner == owner_id
    order = jnp.arange(need_rows.shape[1], dtype=jnp.int32)
    before = order[:, None] < order[None, :]
    ranking = jnp.sum((owned[:, :, None] & before[None]).astype(jnp.int32), axis=1)
    slot_ids = jnp.arange(capacity, dtype=jnp.int32)
    picked = owned[:, :, None] & (ranking[:, :, None] == slot_ids[None, None, :])
    local_ids = jnp.sum(jnp.where(picked, (need_rows % per_owner)[:, :, None], 0), axis=1)
    return (local_ids, jnp.any(picked, axis=1))


def own_ranks(needed, per_owner):
    owners = needed // per_owner
    order = jnp.arange(needed.shape[0], dtype=jnp.int32)
    same_owner = owners[:, None] == owners[None, :]
    before = order[:, None] < order[None, :]
    return (owners, jnp.sum((same_owner & before).astype(jnp.int32), axis=0))


def block_backward(query_rows, grad_rows, key_rows, value_rows, usable):
    scaling = HDIM ** (-0.5)
    query_heads = jnp.moveaxis(query_rows, 2, 0)
    grad_heads = jnp.moveaxis(grad_rows, 2, 0)

    def one_head(totals, pair):
        query_one, grad_one = pair
        scores = (
            jnp.einsum("tkd,skd->kts", query_one, key_rows, preferred_element_type=jnp.float32)
            * scaling
        )
        scores = jnp.where(usable[None, None, :], scores, -jnp.inf)
        row_max = jnp.max(scores, axis=-1, keepdims=True)
        unnormed = jnp.exp(scores - row_max)
        attention = unnormed / jnp.sum(unnormed, axis=-1, keepdims=True)
        attention_low = attention.astype(jnp.bfloat16)
        context = jnp.einsum(
            "kts,skd->tkd", attention_low, value_rows, preferred_element_type=jnp.float32
        )
        context = lax.optimization_barrier(context.astype(jnp.bfloat16))
        row_dot = jnp.sum(context.astype(jnp.float32) * grad_one.astype(jnp.float32), axis=-1)
        grad_attn = jnp.einsum(
            "tkd,skd->kts", grad_one, value_rows, preferred_element_type=jnp.float32
        )
        grad_score = (attention * (grad_attn - jnp.transpose(row_dot, (1, 0))[..., None])).astype(
            jnp.bfloat16
        )
        grad_query = jnp.einsum(
            "kts,skd->tkd", grad_score, key_rows, preferred_element_type=jnp.float32
        )
        key_term = jnp.einsum(
            "kts,tkd->skd", grad_score, query_one, preferred_element_type=jnp.float32
        )
        value_term = jnp.einsum(
            "kts,tkd->skd", attention_low, grad_one, preferred_element_type=jnp.float32
        )
        return (
            (totals[0] + key_term, totals[1] + value_term),
            (grad_query * scaling).astype(jnp.bfloat16),
        )

    empty = jnp.zeros(key_rows.shape, jnp.float32)
    (key_sum, value_sum), query_parts = lax.scan(
        one_head, (empty, empty), (query_heads, grad_heads)
    )
    grad_query = jnp.moveaxis(query_parts, 0, 2)
    return (grad_query, (key_sum * scaling).astype(jnp.bfloat16), value_sum.astype(jnp.bfloat16))


def per_device(queries, image_keys, image_values, out_grad, tile_counts, block_reads):
    seq_count = lax.axis_size("seq")
    my_index = lax.axis_index("seq")
    head_queries, head_grads = (
        lax.all_to_all(queries, "head", split_axis=1, concat_axis=0, tiled=True),
        lax.all_to_all(out_grad, "head", split_axis=1, concat_axis=0, tiled=True),
    )
    per_owner = image_keys.shape[0]
    max_rows = image_keys.shape[1]
    kv_cols = image_keys.shape[2]
    kv_heads = kv_cols // HDIM
    token_rows = head_queries.shape[0]
    group = head_queries.shape[1] // HDIM // kv_heads
    block_count = token_rows // BLK
    need_count = block_count * READS
    width = 2 * SPAN + 1
    capacity = (need_count + 2 * SPAN) // width
    needed = lax.dynamic_slice_in_dim(block_reads, my_index, 1, 0)[0]
    owners, ranking = own_ranks(needed, per_owner)
    local_list = []
    usable_list = []
    bundles = {}
    for offset in range(-SPAN, SPAN + 1):
        reader = (my_index + offset) % seq_count
        row_needs = lax.dynamic_slice_in_dim(block_reads, reader, 1, 0)
        local_row, usable_row = slot_tables(row_needs, my_index, per_owner, capacity)
        local_list.append(local_row[0])
        usable_list.append(usable_row[0])
        bundles[offset] = jnp.stack([image_keys[local_row[0]], image_values[local_row[0]]])
    table_local = jnp.concatenate(local_list)
    table_usable = jnp.concatenate(usable_list)
    received = {0: bundles[0]}
    for offset in range(-SPAN, SPAN + 1):
        if offset != 0:
            received[offset] = passed_along(bundles[offset], "seq", offset)
    got_pairs = jnp.concatenate([received[offset] for offset in range(-SPAN, SPAN + 1)], axis=1)
    flat_keys = got_pairs[0]
    flat_values = got_pairs[1]
    group_ids = (my_index - owners + SPAN) % seq_count
    where_slot = group_ids * capacity + ranking
    need_keys = flat_keys[where_slot].reshape(block_count, READS * max_rows, kv_heads, HDIM)
    need_values = flat_values[where_slot].reshape(block_count, READS * max_rows, kv_heads, HDIM)
    limits = jnp.repeat(tile_counts[needed] * TILE_TOK, max_rows).reshape(
        block_count, READS * max_rows
    )
    positions = jnp.arange(READS * max_rows, dtype=jnp.int32) % max_rows
    usable = positions[None, :] < limits
    query_blocks = head_queries.reshape(block_count, BLK, kv_heads, group, HDIM)
    grad_blocks = head_grads.reshape(block_count, BLK, kv_heads, group, HDIM)
    grad_query, grad_key, grad_value = block_backward(
        query_blocks[0], grad_blocks[0], need_keys[0], need_values[0], usable[0]
    )
    query_list = grad_query.reshape(BLK, group * kv_heads * HDIM)
    key_list = grad_key.reshape(READS, max_rows, kv_cols)
    value_list = grad_value.reshape(READS, max_rows, kv_cols)
    slot_total = flat_keys.shape[0]
    back_keys = (
        jnp.zeros((slot_total, max_rows, kv_cols), jnp.bfloat16).at[where_slot].set(key_list)
    )
    back_values = (
        jnp.zeros((slot_total, max_rows, kv_cols), jnp.bfloat16).at[where_slot].set(value_list)
    )
    back_bundles = {}
    for offset in range(-SPAN, SPAN + 1):
        start = (offset + SPAN) * capacity
        back_bundles[offset] = jnp.stack(
            [back_keys[start : start + capacity], back_values[start : start + capacity]]
        )
    returned = {0: back_bundles[0]}
    for offset in range(-SPAN, SPAN + 1):
        if offset != 0:
            returned[offset] = passed_along(back_bundles[offset], "seq", -offset)
    ret_pairs = jnp.concatenate([returned[offset] for offset in range(-SPAN, SPAN + 1)], axis=1)
    ret_keys = ret_pairs[0]
    ret_values = ret_pairs[1]
    one_hot = (
        (jnp.arange(per_owner, dtype=jnp.int32)[:, None] == table_local[None, :])
        & table_usable[None, :]
    ).astype(jnp.bfloat16)
    key_grad = jnp.einsum("ir,rmc->imc", one_hot, ret_keys, preferred_element_type=jnp.float32)
    value_grad = jnp.einsum("ir,rmc->imc", one_hot, ret_values, preferred_element_type=jnp.float32)
    query_grad = lax.all_to_all(query_list, "head", split_axis=0, concat_axis=1, tiled=True)
    return (query_grad, key_grad.astype(jnp.bfloat16), value_grad.astype(jnp.bfloat16))


def solution(mesh):
    in_specs = (
        P(("seq", "head"), None),
        P("seq", None, "head"),
        P("seq", None, "head"),
        P(("seq", "head"), None),
        P(),
        P(),
    )
    out_specs = (P(("seq", "head"), None), P("seq", None, "head"), P("seq", None, "head"))
    return jax.shard_map(
        per_device, mesh=mesh, in_specs=in_specs, out_specs=out_specs, check_vma=False
    )
```

profile of v0, /device:TPU:1, one launch (start us, length us, event | category | flops | bytes accessed | tf_op | source)
XLA Modules:
  0.0 226.2 jit_solution(437713022074586756)
XLA Ops:
  17.4 4.8 %collective-permute-start.2 = (bf16[2,1,512,128]{3,2,1,0:T(8,128)(2,1)S(1)}, bf16[2,1,512,128]{3,2,1,0:T(8,128)(2,1)S(1)}, u32[]{:S(2)}, u32[]{:S(2)}) collective-permute-start(bf16[2,1,512,128]{3,2,1,0:T(8,128)(2,1)S(1)} %pad_maximum_fusion.7), channel_id=1, source_target_pairs={{508,0},{0,4},{4,8},{8,12},{12,16},{16,20},{20,24},{24,28},{28,32}... | collective-permute-start | bytes 786440 | tf_op jit(solution)/shard_map/ppermute | solution.py:16
  23.0 5.9 %collective-permute-start.1 = (bf16[2,1,512,128]{3,2,1,0:T(8,128)(2,1)}, bf16[2,1,512,128]{3,2,1,0:T(8,128)(2,1)}, u32[]{:S(2)}, u32[]{:S(2)}) collective-permute-start(bf16[2,1,512,128]{3,2,1,0:T(8,128)(2,1)} %pad_maximum_fusion.6), channel_id=1, source_target_pairs={{4,0},{8,4},{12,8},{16,12},{20,16},{24,20},{28,24},{32,28},{36,32}... | collective-permute-start | bytes 786440 | tf_op jit(solution)/shard_map/ppermute | solution.py:16
  29.7 8.2 %collective-permute-start = (bf16[2,1,512,128]{3,2,1,0:T(8,128)(2,1)}, bf16[2,1,512,128]{3,2,1,0:T(8,128)(2,1)}, u32[]{:S(2)}, u32[]{:S(2)}) collective-permute-start(bf16[2,1,512,128]{3,2,1,0:T(8,128)(2,1)} %pad_maximum_fusion.5), channel_id=1, source_target_pairs={{8,0},{12,4},{16,8},{20,12},{24,16},{28,20},{32,24},{36,28},{40,32... | collective-permute-start | bytes 786440 | tf_op jit(solution)/shard_map/ppermute | solution.py:16
  37.9 1.9 collective-permute-start.3
  41.0 4.0 %all-to-all-start = ((bf16[128,4,1024]{2,0,1:T(8,128)(2,1)}), bf16[128,4,1024]{2,0,1:T(8,128)(2,1)S(1)}, u32[]{:S(2)}, u32[]{:S(2)}) async-start(bf16[128,4,1024]{2,0,1:T(8,128)(2,1)} %bitcast.235), calls=%async_computation | async-start | bytes 2097152 | tf_op jit(solution)/shard_map/all_to_all | solution.py:91
  49.0 8.5 %all-to-all-done = bf16[128,4,1024]{2,0,1:T(8,128)(2,1)S(1)} async-done(((bf16[128,4,1024]{2,0,1:T(8,128)(2,1)}), bf16[128,4,1024]{2,0,1:T(8,128)(2,1)S(1)}, u32[]{:S(2)}, u32[]{:S(2)}) %all-to-all-start) | async-done | bytes 1048608 | tf_op jit(solution)/shard_map/all_to_all | solution.py:91
  57.5 3.5 %all-to-all-start.1 = ((bf16[128,4,1024]{2,0,1:T(8,128)(2,1)}), bf16[128,4,1024]{2,0,1:T(8,128)(2,1)S(1)}, u32[]{:S(2)}, u32[]{:S(2)}) async-start(bf16[128,4,1024]{2,0,1:T(8,128)(2,1)} %bitcast.234), calls=%async_computation.1 | async-start | bytes 2097152 | tf_op jit(solution)/shard_map/all_to_all | solution.py:92
  64.1 1.7 gather_fusion.2
  68.5 3.8 %all-to-all-done.1 = bf16[128,4,1024]{2,0,1:T(8,128)(2,1)S(1)} async-done(((bf16[128,4,1024]{2,0,1:T(8,128)(2,1)}), bf16[128,4,1024]{2,0,1:T(8,128)(2,1)S(1)}, u32[]{:S(2)}, u32[]{:S(2)}) %all-to-all-start.1) | async-done | bytes 1048608 | tf_op jit(solution)/shard_map/all_to_all | solution.py:92
  72.7 92.4 %while.25 = (s32[]{:T(128)}, f32[1024,1,128]{0,2,1:T(8,128)}, f32[1024,1,128]{0,2,1:T(8,128)}, bf16[8,512,1,128]{3,1,2,0:T(8,128)(2,1)}, bf16[8,512,1,128]{3,1,2...) while((s32[]{:T(128)}, f32[1024,1,128]{0,2,1:T(8,128)}, ...), condition=%wide.region_15.16_spmd.clone, body=%wide.region_11.15_spmd.clone.sunk | while | flops 814683648 | bytes 30446264 | solution.py:80
  72.9 1.8 fusion.91
  76.4 1.4 multiply_convert_fusion.3
  77.7 2.1 fusion.98
  79.8 2.0 fusion.96
  81.8 2.1 fusion.97
  84.1 1.8 fusion.91
  87.5 1.4 multiply_convert_fusion.3
  88.9 2.1 fusion.98
  91.0 2.2 fusion.96
  93.2 2.3 %fusion.97 = f32[1024,1,128]{0,2,1:T(8,128)} fusion(f32[1024,1,128]{0,2,1:T(8,128)} %get-tuple-element.471, f32[512,1024]{1,0:T(8,128)S(1)} %fusion.93, pred[]{:T(512)S(6)} %compare.60, bf16[8,512,1,128]{3,1,2,0:T(8,128)(2,1)} %copy-done.1, s32[]{:T(128)} %get-tuple-element.469), kind=kOutput, calls=%fused_computation.15.clone.1 | convolution fusion | flops 135004160 | bytes 3277313 | tf_op jit(solution)/shard_map/while/body/eval_jaxpr/kts,tkd->skd/dot_general | solution.py:71
  95.6 1.8 fusion.91
  99.1 1.4 multiply_convert_fusion.3
  100.5 2.1 fusion.98
  102.5 2.2 fusion.96
  104.8 2.3 %fusion.97 = f32[1024,1,128]{0,2,1:T(8,128)} fusion(f32[1024,1,128]{0,2,1:T(8,128)} %get-tuple-element.471, f32[512,1024]{1,0:T(8,128)S(1)} %fusion.93, pred[]{:T(512)S(6)} %compare.60, bf16[8,512,1,128]{3,1,2,0:T(8,128)(2,1)} %copy-done.1, s32[]{:T(128)} %get-tuple-element.469), kind=kOutput, calls=%fused_computation.15.clone.1 | convolution fusion | flops 135004160 | bytes 3277313 | tf_op jit(solution)/shard_map/while/body/eval_jaxpr/kts,tkd->skd/dot_general | solution.py:71
  107.2 1.8 fusion.91
  110.7 1.4 multiply_convert_fusion.3
  112.1 2.1 fusion.98
  114.1 2.2 fusion.96
  116.4 2.3 %fusion.97 = f32[1024,1,128]{0,2,1:T(8,128)} fusion(f32[1024,1,128]{0,2,1:T(8,128)} %get-tuple-element.471, f32[512,1024]{1,0:T(8,128)S(1)} %fusion.93, pred[]{:T(512)S(6)} %compare.60, bf16[8,512,1,128]{3,1,2,0:T(8,128)(2,1)} %copy-done.1, s32[]{:T(128)} %get-tuple-element.469), kind=kOutput, calls=%fused_computation.15.clone.1 | convolution fusion | flops 135004160 | bytes 3277313 | tf_op jit(solution)/shard_map/while/body/eval_jaxpr/kts,tkd->skd/dot_general | solution.py:71
  118.8 1.8 fusion.91
  122.3 1.4 multiply_convert_fusion.3
  123.7 2.1 fusion.98
  125.7 2.2 fusion.96
  128.0 2.3 %fusion.97 = f32[1024,1,128]{0,2,1:T(8,128)} fusion(f32[1024,1,128]{0,2,1:T(8,128)} %get-tuple-element.471, f32[512,1024]{1,0:T(8,128)S(1)} %fusion.93, pred[]{:T(512)S(6)} %compare.60, bf16[8,512,1,128]{3,1,2,0:T(8,128)(2,1)} %copy-done.1, s32[]{:T(128)} %get-tuple-element.469), kind=kOutput, calls=%fused_computation.15.clone.1 | convolution fusion | flops 135004160 | bytes 3277313 | tf_op jit(solution)/shard_map/while/body/eval_jaxpr/kts,tkd->skd/dot_general | solution.py:71
  130.4 1.8 fusion.91
  133.9 1.4 multiply_convert_fusion.3
  135.3 2.1 fusion.98
  137.3 2.2 fusion.96
  139.6 2.3 %fusion.97 = f32[1024,1,128]{0,2,1:T(8,128)} fusion(f32[1024,1,128]{0,2,1:T(8,128)} %get-tuple-element.471, f32[512,1024]{1,0:T(8,128)S(1)} %fusion.93, pred[]{:T(512)S(6)} %compare.60, bf16[8,512,1,128]{3,1,2,0:T(8,128)(2,1)} %copy-done.1, s32[]{:T(128)} %get-tuple-element.469), kind=kOutput, calls=%fused_computation.15.clone.1 | convolution fusion | flops 135004160 | bytes 3277313 | tf_op jit(solution)/shard_map/while/body/eval_jaxpr/kts,tkd->skd/dot_general | solution.py:71
  142.0 1.8 fusion.91
  145.5 1.4 multiply_convert_fusion.3
  146.9 2.1 fusion.98
  148.9 2.2 fusion.96
  151.2 2.3 %fusion.97 = f32[1024,1,128]{0,2,1:T(8,128)} fusion(f32[1024,1,128]{0,2,1:T(8,128)} %get-tuple-element.471, f32[512,1024]{1,0:T(8,128)S(1)} %fusion.93, pred[]{:T(512)S(6)} %compare.60, bf16[8,512,1,128]{3,1,2,0:T(8,128)(2,1)} %copy-done.1, s32[]{:T(128)} %get-tuple-element.469), kind=kOutput, calls=%fused_computation.15.clone.1 | convolution fusion | flops 135004160 | bytes 3277313 | tf_op jit(solution)/shard_map/while/body/eval_jaxpr/kts,tkd->skd/dot_general | solution.py:71
  153.6 1.8 fusion.91
  157.1 1.4 multiply_convert_fusion.3
  158.5 2.1 fusion.98
  160.5 2.2 fusion.96
  162.8 2.3 %fusion.97 = f32[1024,1,128]{0,2,1:T(8,128)} fusion(f32[1024,1,128]{0,2,1:T(8,128)} %get-tuple-element.471, f32[512,1024]{1,0:T(8,128)S(1)} %fusion.93, pred[]{:T(512)S(6)} %compare.60, bf16[8,512,1,128]{3,1,2,0:T(8,128)(2,1)} %copy-done.1, s32[]{:T(128)} %get-tuple-element.469), kind=kOutput, calls=%fused_computation.15.clone.1 | convolution fusion | flops 135004160 | bytes 3277313 | tf_op jit(solution)/shard_map/while/body/eval_jaxpr/kts,tkd->skd/dot_general | solution.py:71
  170.6 6.1 %collective-permute-start.7 = (bf16[2,1,512,128]{3,1,2,0:T(2,128)(2,1)S(1)}, bf16[2,1,512,128]{3,1,2,0:T(2,128)(2,1)S(1)}, u32[]{:S(2)}, u32[]{:S(2)}) collective-permute-start(bf16[2,1,512,128]{3,1,2,0:T(2,128)(2,1)S(1)} %pad_maximum_fusion.4), channel_id=1, source_target_pairs={{8,0},{12,4},{16,8},{20,12},{24,16},{28,20},{32,24},{36,28},{40,32... | collective-permute-start | bytes 786440 | tf_op jit(solution)/shard_map/ppermute | solution.py:16
  177.1 1.7 pad_maximum_fusion.3
  178.8 7.2 %collective-permute-start.6 = (bf16[2,1,512,128]{3,1,2,0:T(2,128)(2,1)}, bf16[2,1,512,128]{3,1,2,0:T(2,128)(2,1)S(1)}, u32[]{:S(2)}, u32[]{:S(2)}) collective-permute-start(bf16[2,1,512,128]{3,1,2,0:T(2,128)(2,1)} %pad_maximum_fusion.3), channel_id=1, source_target_pairs={{4,0},{8,4},{12,8},{16,12},{20,16},{24,20},{28,24},{32,28},{36,32}... | collective-permute-start | bytes 786440 | tf_op jit(solution)/shard_map/ppermute | solution.py:16
  186.4 1.7 pad_maximum_fusion.1
  188.1 2.1 collective-permute-start.5
  190.6 1.7 pad_maximum_fusion
  192.3 1.9 collective-permute-start.4
  194.2 1.9 copy.277
  197.4 3.5 %all-to-all-start.2 = ((bf16[4,128,1024]{2,1,0:T(8,128)(2,1)}), bf16[4,128,1024]{2,1,0:T(8,128)(2,1)S(1)}, u32[]{:S(2)}, u32[]{:S(2)}) async-start(bf16[4,128,1024]{2,1,0:T(8,128)(2,1)} %all_to_all.44), calls=%async_computation.2 | async-start | bytes 2097152 | tf_op jit(solution)/shard_map/all_to_all | solution.py:168
  201.6 3.1 %concatenate.13 = s32[5]{0:T(128)S(1)} concatenate(s32[1]{0:T(128)} %bitcast.4, s32[1]{0:T(128)} %bitcast.10, s32[1]{0:T(128)} %bitcast.16, s32[1]{0:T(128)} %bitcast.22, s32[1]{0:T(128)} %bitcast.28), dimensions={0} | concatenate | bytes 40 | tf_op jit(solution)/shard_map/concatenate | solution.py:116
  205.4 3.3 %concatenate.14 = pred[5]{0:T(512)(128)(4,1)S(1)} concatenate(pred[1]{0:T(512)(128)(4,1)} %bitcast.47, pred[1]{0:T(512)(128)(4,1)} %bitcast.48, pred[1]{0:T(512)(128)(4,1)} %bitcast.49, pred[1]{0:T(512)(128)(4,1)} %bitcast.50, pred[1]{0:T(512)(128)(4,1)} %bitcast.51), dimensions={0} | concatenate | bytes 10 | tf_op jit(solution)/shard_map/concatenate | solution.py:117
  209.0 1.7 pad_maximum_fusion.2
  212.8 8.9 %concatenate.15 = bf16[2,5,512,128]{3,1,2,0:T(8,128)(2,1)S(1)} concatenate(bf16[2,1,512,128]{3,1,2,0:T(2,128)(2,1)} %collective-permute-done.4, bf16[2,1,512,128]{3,1,2,0:T(2,128)(2,1)} %copy-done.7, bf16[2,1,512,128]{3,1,2,0:T(2,128)(2,1)} %pad_maximum_fusion.2, bf16[2,1,512,128]{3,1,2,0:T(2,128)(2,1)} %copy-done.6, bf16[2,1,512,128]{3,1,2,0:T(2,128)(2,1)} %copy-done.5), dimensions={1} | concatenate | bytes 2621440 | tf_op jit(solution)/shard_map/concatenate | solution.py:159
  224.9 1.3 copy.291
  (194 shorter events, 49.5 us)
Async XLA Ops:
  0.6 44.6 %copy-start = (s32[512]{0:T(512)S(1)}, s32[512]{0:T(512)}, u32[]{:S(2)}) copy-start(s32[512]{0:T(512)} %param.12) | copy-start | bytes 6148
  10.2 19.5 %copy-start.8 = (s32[2]{0:T(128)}, s32[2]{0:T(128)S(1)}, u32[]{:S(2)}) copy-start(s32[2]{0:T(128)S(1)} %fusion.37) | copy-start | bytes 28
  14.9 25.0 %copy-start.3 = (bf16[128,4096]{1,0:T(8,128)(2,1)S(1)}, bf16[128,4096]{1,0:T(8,128)(2,1)}, u32[]{:S(2)}) copy-start(bf16[128,4096]{1,0:T(8,128)(2,1)} %param.8) | copy-start | bytes 3145732
  17.4 45.6 %collective-permute-start.2 = (bf16[2,1,512,128]{3,2,1,0:T(8,128)(2,1)S(1)}, bf16[2,1,512,128]{3,2,1,0:T(8,128)(2,1)S(1)}, u32[]{:S(2)}, u32[]{:S(2)}) collective-permute-start(bf16[2,1,512,128]{3,2,1,0:T(8,128)(2,1)S(1)} %pad_maximum_fusion.7), channel_id=1, source_target_pairs={{508,0},{0,4},{4,8},{8,12},{12,16},{16,20},{20,24},{24,28},{28,32}... | collective-permute-start | bytes 786440 | tf_op jit(solution)/shard_map/ppermute | solution.py:16
  23.0 39.0 %collective-permute-start.1 = (bf16[2,1,512,128]{3,2,1,0:T(8,128)(2,1)}, bf16[2,1,512,128]{3,2,1,0:T(8,128)(2,1)}, u32[]{:S(2)}, u32[]{:S(2)}) collective-permute-start(bf16[2,1,512,128]{3,2,1,0:T(8,128)(2,1)} %pad_maximum_fusion.6), channel_id=1, source_target_pairs={{4,0},{8,4},{12,8},{16,12},{20,16},{24,20},{28,24},{32,28},{36,32}... | collective-permute-start | bytes 786440 | tf_op jit(solution)/shard_map/ppermute | solution.py:16
  29.7 31.3 %collective-permute-start = (bf16[2,1,512,128]{3,2,1,0:T(8,128)(2,1)}, bf16[2,1,512,128]{3,2,1,0:T(8,128)(2,1)}, u32[]{:S(2)}, u32[]{:S(2)}) collective-permute-start(bf16[2,1,512,128]{3,2,1,0:T(8,128)(2,1)} %pad_maximum_fusion.5), channel_id=1, source_target_pairs={{8,0},{12,4},{16,8},{20,12},{24,16},{28,20},{32,24},{36,28},{40,32... | collective-permute-start | bytes 786440 | tf_op jit(solution)/shard_map/ppermute | solution.py:16
  37.9 25.2 %collective-permute-start.3 = (bf16[2,1,512,128]{3,2,1,0:T(8,128)(2,1)S(1)}, bf16[2,1,512,128]{3,2,1,0:T(8,128)(2,1)S(1)}, u32[]{:S(2)}, u32[]{:S(2)}) collective-permute-start(bf16[2,1,512,128]{3,2,1,0:T(8,128)(2,1)S(1)} %pad_maximum_fusion.8), channel_id=1, source_target_pairs={{504,0},{508,4},{0,8},{4,12},{8,16},{12,20},{16,24},{20,28},{24,32... | collective-permute-start | bytes 786440 | tf_op jit(solution)/shard_map/ppermute | solution.py:16
  39.9 7.3 %copy-start.4 = (bf16[128,4096]{1,0:T(8,128)(2,1)S(1)}, bf16[128,4096]{1,0:T(8,128)(2,1)}, u32[]{:S(2)}) copy-start(bf16[128,4096]{1,0:T(8,128)(2,1)} %param.11) | copy-start | bytes 3145732
  41.0 16.6 %all-to-all-start = ((bf16[128,4,1024]{2,0,1:T(8,128)(2,1)}), bf16[128,4,1024]{2,0,1:T(8,128)(2,1)S(1)}, u32[]{:S(2)}, u32[]{:S(2)}) async-start(bf16[128,4,1024]{2,0,1:T(8,128)(2,1)} %bitcast.235), calls=%async_computation | async-start | bytes 2097152 | tf_op jit(solution)/shard_map/all_to_all | solution.py:91
  57.5 14.8 %all-to-all-start.1 = ((bf16[128,4,1024]{2,0,1:T(8,128)(2,1)}), bf16[128,4,1024]{2,0,1:T(8,128)(2,1)S(1)}, u32[]{:S(2)}, u32[]{:S(2)}) async-start(bf16[128,4,1024]{2,0,1:T(8,128)(2,1)} %bitcast.234), calls=%async_computation.1 | async-start | bytes 2097152 | tf_op jit(solution)/shard_map/all_to_all | solution.py:92
  72.8 3.4 %copy-start.1 = (bf16[8,512,1,128]{3,1,2,0:T(8,128)(2,1)}, bf16[8,512,1,128]{3,1,2,0:T(8,128)(2,1)S(1)}, u32[]{:S(2)}) copy-start(bf16[8,512,1,128]{3,1,2,0:T(8,128)(2,1)S(1)} %get-tuple-element.486) | copy-start | bytes 3145732 | tf_op jit(solution)/shard_map/while
  81.8 2.1 copy-start.2
  83.9 3.4 %copy-start.1 = (bf16[8,512,1,128]{3,1,2,0:T(8,128)(2,1)}, bf16[8,512,1,128]{3,1,2,0:T(8,128)(2,1)S(1)}, u32[]{:S(2)}) copy-start(bf16[8,512,1,128]{3,1,2,0:T(8,128)(2,1)S(1)} %get-tuple-element.486) | copy-start | bytes 3145732 | tf_op jit(solution)/shard_map/while
  93.2 2.3 %copy-start.2 = (bf16[8,512,1,128]{3,1,2,0:T(8,128)(2,1)S(1)}, bf16[8,512,1,128]{3,1,2,0:T(8,128)(2,1)}, u32[]{:S(2)}) copy-start(bf16[8,512,1,128]{3,1,2,0:T(8,128)(2,1)} %copy-done.1) | copy-start | bytes 3145732 | tf_op jit(solution)/shard_map/while
  95.5 3.4 %copy-start.1 = (bf16[8,512,1,128]{3,1,2,0:T(8,128)(2,1)}, bf16[8,512,1,128]{3,1,2,0:T(8,128)(2,1)S(1)}, u32[]{:S(2)}) copy-start(bf16[8,512,1,128]{3,1,2,0:T(8,128)(2,1)S(1)} %get-tuple-element.486) | copy-start | bytes 3145732 | tf_op jit(solution)/shard_map/while
  104.8 2.3 %copy-start.2 = (bf16[8,512,1,128]{3,1,2,0:T(8,128)(2,1)S(1)}, bf16[8,512,1,128]{3,1,2,0:T(8,128)(2,1)}, u32[]{:S(2)}) copy-start(bf16[8,512,1,128]{3,1,2,0:T(8,128)(2,1)} %copy-done.1) | copy-start | bytes 3145732 | tf_op jit(solution)/shard_map/while
  107.1 3.4 %copy-start.1 = (bf16[8,512,1,128]{3,1,2,0:T(8,128)(2,1)}, bf16[8,512,1,128]{3,1,2,0:T(8,128)(2,1)S(1)}, u32[]{:S(2)}) copy-start(bf16[8,512,1,128]{3,1,2,0:T(8,128)(2,1)S(1)} %get-tuple-element.486) | copy-start | bytes 3145732 | tf_op jit(solution)/shard_map/while
  116.4 2.3 %copy-start.2 = (bf16[8,512,1,128]{3,1,2,0:T(8,128)(2,1)S(1)}, bf16[8,512,1,128]{3,1,2,0:T(8,128)(2,1)}, u32[]{:S(2)}) copy-start(bf16[8,512,1,128]{3,1,2,0:T(8,128)(2,1)} %copy-done.1) | copy-start | bytes 3145732 | tf_op jit(solution)/shard_map/while
  118.7 3.4 %copy-start.1 = (bf16[8,512,1,128]{3,1,2,0:T(8,128)(2,1)}, bf16[8,512,1,128]{3,1,2,0:T(8,128)(2,1)S(1)}, u32[]{:S(2)}) copy-start(bf16[8,512,1,128]{3,1,2,0:T(8,128)(2,1)S(1)} %get-tuple-element.486) | copy-start | bytes 3145732 | tf_op jit(solution)/shard_map/while
  128.0 2.3 %copy-start.2 = (bf16[8,512,1,128]{3,1,2,0:T(8,128)(2,1)S(1)}, bf16[8,512,1,128]{3,1,2,0:T(8,128)(2,1)}, u32[]{:S(2)}) copy-start(bf16[8,512,1,128]{3,1,2,0:T(8,128)(2,1)} %copy-done.1) | copy-start | bytes 3145732 | tf_op jit(solution)/shard_map/while
  130.3 3.4 %copy-start.1 = (bf16[8,512,1,128]{3,1,2,0:T(8,128)(2,1)}, bf16[8,512,1,128]{3,1,2,0:T(8,128)(2,1)S(1)}, u32[]{:S(2)}) copy-start(bf16[8,512,1,128]{3,1,2,0:T(8,128)(2,1)S(1)} %get-tuple-element.486) | copy-start | bytes 3145732 | tf_op jit(solution)/shard_map/while
  139.6 2.3 %copy-start.2 = (bf16[8,512,1,128]{3,1,2,0:T(8,128)(2,1)S(1)}, bf16[8,512,1,128]{3,1,2,0:T(8,128)(2,1)}, u32[]{:S(2)}) copy-start(bf16[8,512,1,128]{3,1,2,0:T(8,128)(2,1)} %copy-done.1) | copy-start | bytes 3145732 | tf_op jit(solution)/shard_map/while
  141.9 3.4 %copy-start.1 = (bf16[8,512,1,128]{3,1,2,0:T(8,128)(2,1)}, bf16[8,512,1,128]{3,1,2,0:T(8,128)(2,1)S(1)}, u32[]{:S(2)}) copy-start(bf16[8,512,1,128]{3,1,2,0:T(8,128)(2,1)S(1)} %get-tuple-element.486) | copy-start | bytes 3145732 | tf_op jit(solution)/shard_map/while
  151.2 2.3 %copy-start.2 = (bf16[8,512,1,128]{3,1,2,0:T(8,128)(2,1)S(1)}, bf16[8,512,1,128]{3,1,2,0:T(8,128)(2,1)}, u32[]{:S(2)}) copy-start(bf16[8,512,1,128]{3,1,2,0:T(8,128)(2,1)} %copy-done.1) | copy-start | bytes 3145732 | tf_op jit(solution)/shard_map/while
  153.5 3.4 %copy-start.1 = (bf16[8,512,1,128]{3,1,2,0:T(8,128)(2,1)}, bf16[8,512,1,128]{3,1,2,0:T(8,128)(2,1)S(1)}, u32[]{:S(2)}) copy-start(bf16[8,512,1,128]{3,1,2,0:T(8,128)(2,1)S(1)} %get-tuple-element.486) | copy-start | bytes 3145732 | tf_op jit(solution)/shard_map/while
  162.8 2.3 %copy-start.2 = (bf16[8,512,1,128]{3,1,2,0:T(8,128)(2,1)S(1)}, bf16[8,512,1,128]{3,1,2,0:T(8,128)(2,1)}, u32[]{:S(2)}) copy-start(bf16[8,512,1,128]{3,1,2,0:T(8,128)(2,1)} %copy-done.1) | copy-start | bytes 3145732 | tf_op jit(solution)/shard_map/while
  170.6 40.1 %collective-permute-start.7 = (bf16[2,1,512,128]{3,1,2,0:T(2,128)(2,1)S(1)}, bf16[2,1,512,128]{3,1,2,0:T(2,128)(2,1)S(1)}, u32[]{:S(2)}, u32[]{:S(2)}) collective-permute-start(bf16[2,1,512,128]{3,1,2,0:T(2,128)(2,1)S(1)} %pad_maximum_fusion.4), channel_id=1, source_target_pairs={{8,0},{12,4},{16,8},{20,12},{24,16},{28,20},{32,24},{36,28},{40,32... | collective-permute-start | bytes 786440 | tf_op jit(solution)/shard_map/ppermute | solution.py:16
  178.8 31.9 %collective-permute-start.6 = (bf16[2,1,512,128]{3,1,2,0:T(2,128)(2,1)}, bf16[2,1,512,128]{3,1,2,0:T(2,128)(2,1)S(1)}, u32[]{:S(2)}, u32[]{:S(2)}) collective-permute-start(bf16[2,1,512,128]{3,1,2,0:T(2,128)(2,1)} %pad_maximum_fusion.3), channel_id=1, source_target_pairs={{4,0},{8,4},{12,8},{16,12},{20,16},{24,20},{28,24},{32,28},{36,32}... | collective-permute-start | bytes 786440 | tf_op jit(solution)/shard_map/ppermute | solution.py:16
  188.1 22.6 %collective-permute-start.5 = (bf16[2,1,512,128]{3,1,2,0:T(2,128)(2,1)}, bf16[2,1,512,128]{3,1,2,0:T(2,128)(2,1)S(1)}, u32[]{:S(2)}, u32[]{:S(2)}) collective-permute-start(bf16[2,1,512,128]{3,1,2,0:T(2,128)(2,1)} %pad_maximum_fusion.1), channel_id=1, source_target_pairs={{508,0},{0,4},{4,8},{8,12},{12,16},{16,20},{20,24},{24,28},{28,32}... | collective-permute-start | bytes 786440 | tf_op jit(solution)/shard_map/ppermute | solution.py:16
  192.3 20.5 %collective-permute-start.4 = (bf16[2,1,512,128]{3,1,2,0:T(2,128)(2,1)}, bf16[2,1,512,128]{3,1,2,0:T(2,128)(2,1)}, u32[]{:S(2)}, u32[]{:S(2)}) collective-permute-start(bf16[2,1,512,128]{3,1,2,0:T(2,128)(2,1)} %pad_maximum_fusion), channel_id=1, source_target_pairs={{504,0},{508,4},{0,8},{4,12},{8,16},{12,20},{16,24},{20,28},{24,32... | collective-permute-start | bytes 786440 | tf_op jit(solution)/shard_map/ppermute | solution.py:16
  196.1 4.8 %copy-start.9 = (s32[2]{0:T(128)S(1)}, s32[2]{0:T(128)}, u32[]{:S(2)}) copy-start(s32[2]{0:T(128)} %copy-done.8) | copy-start | bytes 28
  197.4 26.9 %all-to-all-start.2 = ((bf16[4,128,1024]{2,1,0:T(8,128)(2,1)}), bf16[4,128,1024]{2,1,0:T(8,128)(2,1)S(1)}, u32[]{:S(2)}, u32[]{:S(2)}) async-start(bf16[4,128,1024]{2,1,0:T(8,128)(2,1)} %all_to_all.44), calls=%async_computation.2 | async-start | bytes 2097152 | tf_op jit(solution)/shard_map/all_to_all | solution.py:168
  210.7 0.8 copy-start.5
  210.7 1.0 copy-start.6
  211.7 0.8 copy-start.7
where the time goes:
time: 229 us; the launch traced here: 226 us
  matrix products  82.3 us (36%)
  starting transfers between devices  49.2 us (21%)
  local copies, waits for them, and re-layouts  43.2 us (19%)
  other arithmetic  28.4 us (12%)
  waiting for transfers between devices  12.6 us (6%)
  between operations  10.2 us (4%)
    ppermute x8, starting transfers between devices, passed_along(): return lax.ppermute(block, axis, route)  38.2 us
    dot_general x8, matrix products, one_head(): jnp.einsum('kts,tkd->skd', attention_low, grad_one, preferred_element_typ...  18.4 us
    dot_general x8, matrix products, one_head(): jnp.einsum('kts,tkd->skd', grad_score, query_one, preferred_element_type=...  17.8 us
    dot_general x8, matrix products, one_head(): jnp.einsum('kts,skd->tkd', grad_score, key_rows, preferred_element_type=j...  16.4 us
    dot_general x8, matrix products, one_head(): jnp.einsum('tkd,skd->kts', query_one, key_rows, preferred_element_type=jn...  14.5 us
    dot_general x8, matrix products, one_head(): jnp.einsum('tkd,skd->kts', grad_one, value_rows, preferred_element_type=j...  10.8 us
    unnamed x32, local copies, waits for them, and re-layouts  9.22 us
    concatenate x1, local copies, waits for them, and re-layouts, per_device(): jnp.concatenate([returned[offset] for offset in range(-SPAN, SPAN + 1)],...  8.89 us
  transfers between devices with their start and end apart: 11, of which 3 were waited for; matrix products, arithmetic and copies ran while one was open for 19% of the time, Pallas kernels for 0%

commit v1 on v0

v1 whole, which is shorter than its diff:
```python
import functools

import jax
import jax.numpy as jnp
from jax import lax
from jax.experimental import pallas as pl
from jax.experimental.pallas import tpu as pltpu
from jax.sharding import PartitionSpec as P

HDIM = 128
TILE = 128
READS = 2
SPAN = 2
WIDTH = 2 * SPAN + 1
SCALE = HDIM ** (-0.5)
SCALE2 = SCALE * 1.4426950408889634
UNIT = 256
PAIRS = UNIT // HDIM
F32 = jnp.float32
BF16 = jnp.bfloat16
MESH = pl.DeviceIdType.MESH
NN = (((1,), (0,)), ((), ()))
NT = (((1,), (1,)), ((), ()))
HOPS = (1, 3, 2)


def dot(a, b, dims):
    return lax.dot_general(a, b, dims, preferred_element_type=F32)


def heads_to_rows(x):
    return jnp.concatenate([x[:, h * HDIM : (h + 1) * HDIM] for h in range(PAIRS)], axis=0)


def kernel(
    sizes,
    counts_ref,
    reads_ref,
    q_hbm,
    k_hbm,
    v_hbm,
    g_hbm,
    dq_hbm,
    dk_hbm,
    dv_hbm,
    own_k,
    own_v,
    put_k,
    put_v,
    got_k,
    got_v,
    ret_k,
    ret_v,
    q_all,
    g_all,
    dq_all,
    keys,
    keys_t,
    values,
    s0,
    d0,
    s1,
    d1,
    att,
    dsc,
    row_max,
    sum_k,
    sum_v,
    low_k,
    low_v,
    out_k,
    out_v,
    own_sem,
    q_sem,
    g_sem,
    qs_sem,
    gs_sem,
    kv_send,
    kv_recv,
    back_send,
    back_recv,
    dq_send,
    dq_recv,
    out_sem,
):
    n_seq, n_head, per_owner, slots, head_cols = sizes
    per_head = head_cols // UNIT
    units = n_head * per_head
    n_tiles = READS * slots // TILE
    tiles = slots // TILE
    s = lax.axis_index("seq")
    x = lax.axis_index("head")

    def along_head(k):
        return lax.rem(x + k, n_head)

    def along_seq(o):
        return lax.rem(s + o + n_seq, n_seq)

    load_k = pltpu.make_async_copy(k_hbm, own_k, own_sem.at[0])
    load_v = pltpu.make_async_copy(v_hbm, own_v, own_sem.at[1])
    load_k.start()
    load_v.start()

    def own_load(u):
        cols = pl.ds(pl.multiple_of(x * head_cols + u * UNIT, UNIT), UNIT)
        return (
            pltpu.make_async_copy(q_hbm.at[:, cols], q_all.at[u], q_sem.at[u]),
            pltpu.make_async_copy(g_hbm.at[:, cols], g_all.at[u], g_sem.at[u]),
        )

    for u in range(per_head):
        for c in own_load(u):
            c.start()

    barrier = pltpu.get_barrier_semaphore()
    offsets = [o for o in range(-SPAN, SPAN + 1) if o != 0]
    for k in range(1, n_head):
        pl.semaphore_signal(barrier, inc=1, device_id=(s, along_head(k)), device_id_type=MESH)
    for o in offsets:
        pl.semaphore_signal(barrier, inc=1, device_id=(along_seq(o), x), device_id_type=MESH)
    pl.semaphore_wait(barrier, n_head - 1 + len(offsets))

    picks = []
    for o in range(-SPAN, SPAN + 1):
        reader = along_seq(o)
        first = reads_ref[reader, 0] - s * per_owner
        second = reads_ref[reader, 1] - s * per_owner
        one = (first >= 0) & (first < per_owner)
        two = (second >= 0) & (second < per_owner)
        picks.append(jnp.where(one, first, jnp.where(two, second, 0)))

    def kv_copy(put, got, o, kind):
        g = o + SPAN
        return pltpu.make_async_remote_copy(
            src_ref=put.at[g],
            dst_ref=got.at[g],
            send_sem=kv_send.at[kind, g],
            recv_sem=kv_recv.at[kind, g],
            device_id=(along_seq(o), x),
            device_id_type=MESH,
        )

    load_k.wait()
    for o in offsets:
        put_k[o + SPAN] = own_k[picks[o + SPAN]]
        kv_copy(put_k, got_k, o, 0).start()
    got_k[SPAN] = own_k[picks[SPAN]]
    load_v.wait()
    for o in offsets:
        put_v[o + SPAN] = own_v[picks[o + SPAN]]
        kv_copy(put_v, got_v, o, 1).start()
    got_v[SPAN] = own_v[picks[SPAN]]

    def share_copy(i, k, src, dst, ssem, rsem):
        u = per_head + (n_head - 1) * i + HOPS.index(k)
        to = along_head(k)
        cols = pl.ds(pl.multiple_of(to * head_cols + i * UNIT, UNIT), UNIT)
        return pltpu.make_async_remote_copy(
            src_ref=src.at[:, cols],
            dst_ref=dst.at[u],
            send_sem=ssem.at[u],
            recv_sem=rsem.at[u],
            device_id=(s, to),
            device_id_type=MESH,
        )

    shares = []
    for i in range(per_head):
        for k in HOPS:
            shares.append(share_copy(i, k, q_hbm, q_all, qs_sem, q_sem))
            shares.append(share_copy(i, k, g_hbm, g_all, gs_sem, g_sem))
    for c in shares:
        c.start()

    def await_share(u):
        for buf, ssem, rsem in ((q_all, qs_sem, q_sem), (g_all, gs_sem, g_sem)):
            pltpu.make_async_remote_copy(
                src_ref=buf.at[u],
                dst_ref=buf.at[u],
                send_sem=ssem.at[u],
                recv_sem=rsem.at[u],
                device_id=(s, along_head(1)),
                device_id_type=MESH,
            ).wait_recv()

    images = [reads_ref[s, j] for j in range(READS)]
    groups = [
        jnp.minimum(lax.rem(s - (images[j] // per_owner) + SPAN + n_seq, n_seq), WIDTH - 1)
        for j in range(READS)
    ]
    limits = [counts_ref[images[j]] for j in range(READS)]
    sum_k[...] = jnp.zeros_like(sum_k)
    sum_v[...] = jnp.zeros_like(sum_v)
    for u in range(per_head):
        for c in own_load(u):
            c.wait()
    for o in offsets:
        kv_copy(put_k, got_k, o, 0).wait()
    for j in range(READS):
        keys[j * slots : (j + 1) * slots, :] = got_k[groups[j]]
    keys_t[...] = keys[...].T
    for o in offsets:
        kv_copy(put_v, got_v, o, 1).wait()
    for j in range(READS):
        values[j * slots : (j + 1) * slots, :] = got_v[groups[j]]

    def usable(i):
        return (i % tiles) < limits[i // tiles]

    chunk = 512
    n_chunks = READS * slots // chunk
    chunk_tiles = chunk // TILE
    halves = ((s0, d0), (s1, d1))

    def score_chunk(q, g, half, c):
        s_ref, d_ref = half
        rows = pl.ds(c * chunk, chunk)
        score = dot(keys[rows, :], q, NT)
        s_ref[rows, :] = score
        d_ref[rows, :] = dot(values[rows, :], g, NT)
        return [
            jnp.max(score[t * TILE : (t + 1) * TILE].reshape(TILE // 8, 8, UNIT), axis=0)
            for t in range(chunk_tiles)
        ]

    def finish_max(tops):
        top = None
        for i in range(n_tiles):
            one = jnp.where(usable(i), tops[i], -jnp.inf)
            top = one if top is None else jnp.maximum(top, one)
        return jnp.max(top, axis=0, keepdims=True) * SCALE2

    def first_scores():
        q, g = heads_to_rows(q_all[0]), heads_to_rows(g_all[0])
        tops = []
        for c in range(n_chunks):
            tops += score_chunk(q, g, halves[0], c)
        row_max[0:1, :] = finish_max(tops)

    def step(u, b, more):
        s_ref, d_ref = halves[b]
        top = row_max[b : b + 1, :]
        total = jnp.zeros((8, UNIT), F32)
        weighted = jnp.zeros((8, UNIT), F32)
        tops = []
        if more:
            qn, gn = heads_to_rows(q_all[u + 1]), heads_to_rows(g_all[u + 1])
        for c in range(n_chunks):
            if more:
                tops += score_chunk(qn, gn, halves[1 - b], c)
            for t in range(chunk_tiles):
                i = c * chunk_tiles + t
                rows = pl.ds(i * TILE, TILE)
                shift = jnp.where(usable(i), top, jnp.inf)
                p = jnp.exp2(s_ref[rows, :] * SCALE2 - shift)
                s_ref[rows, :] = p
                total = total + jnp.sum(p.reshape(TILE // 8, 8, UNIT), axis=0)
                weighted = weighted + jnp.sum(
                    (p * d_ref[rows, :]).reshape(TILE // 8, 8, UNIT), axis=0
                )
        if more:
            row_max[1 - b : 2 - b, :] = finish_max(tops)
        inverse = 1.0 / jnp.sum(total, axis=0, keepdims=True)
        row_dot = jnp.sum(weighted, axis=0, keepdims=True) * inverse
        q, g = heads_to_rows(q_all[u]), heads_to_rows(g_all[u])
        dq = None
        for c in range(n_chunks):
            for t in range(chunk_tiles):
                rows = pl.ds((c * chunk_tiles + t) * TILE, TILE)
                a = s_ref[rows, :] * inverse
                att[rows, :] = a.astype(BF16)
                dsc[rows, :] = (a * (d_ref[rows, :] - row_dot)).astype(BF16)
            rows = pl.ds(c * chunk, chunk)
            sum_v[rows, :] += dot(att[rows, :], g, NN)
            sum_k[rows, :] += dot(dsc[rows, :], q, NN)
            part = dot(keys_t[:, c * chunk : (c + 1) * chunk], dsc[rows, :], NN)
            dq = part if dq is None else dq + part
        dq = (dq * SCALE).T.astype(BF16)
        for h in range(PAIRS):
            dq_all[u, :, h * HDIM : (h + 1) * HDIM] = dq[h * HDIM : (h + 1) * HDIM]

    def dq_own(u):
        cols = pl.ds(pl.multiple_of(x * head_cols + u * UNIT, UNIT), UNIT)
        return pltpu.make_async_copy(dq_all.at[u], dq_hbm.at[:, cols], dq_send.at[u])

    def dq_copy(u):
        r = u - per_head
        i = lax.div(r, n_head - 1)
        h = lax.rem(r, n_head - 1)
        hop = jnp.where(h == 0, HOPS[0], jnp.where(h == 1, HOPS[1], HOPS[2]))
        cols = pl.ds(pl.multiple_of(x * head_cols + i * UNIT, UNIT), UNIT)
        return pltpu.make_async_remote_copy(
            src_ref=dq_all.at[u],
            dst_ref=dq_hbm.at[:, cols],
            send_sem=dq_send.at[u],
            recv_sem=dq_recv.at[u],
            device_id=(s, lax.rem(x - hop + n_head, n_head)),
            device_id_type=MESH,
        )

    first_scores()
    for u in range(per_head - 1):
        step(u, u % 2, True)
        dq_own(u).start()
    await_share(per_head)
    step(per_head - 1, (per_head - 1) % 2, True)
    dq_own(per_head - 1).start()

    def two(j, carry):
        u = per_head + 2 * j
        await_share(u + 1)
        step(u, 0, True)
        dq_copy(u).start()
        await_share(u + 2)
        step(u + 1, 1, True)
        dq_copy(u + 1).start()
        return carry

    lax.fori_loop(0, (units - per_head) // 2 - 1, two, 0)
    await_share(units - 1)
    step(units - 2, 0, True)
    dq_copy(units - 2).start()
    step(units - 1, 1, False)
    dq_copy(units - 1).start()

    def back_copy(put, got, o, kind):
        g = o + SPAN
        return pltpu.make_async_remote_copy(
            src_ref=put.at[g],
            dst_ref=got.at[g],
            send_sem=back_send.at[kind, g],
            recv_sem=back_recv.at[kind, g],
            device_id=(along_seq(-o), x),
            device_id_type=MESH,
        )

    which = []
    for g in range(WIDTH):
        which.append(jnp.where(groups[0] == g, 0, jnp.where(groups[1] == g, 1, READS)))
    for low, total, factor, put, got, kind in (
        (low_v, sum_v, None, put_v, ret_v, 1),
        (low_k, sum_k, SCALE, put_k, ret_k, 0),
    ):
        for j in range(READS):
            block = total[j * slots : (j + 1) * slots, :]
            low[j] = (block if factor is None else block * factor).astype(BF16)
        low[READS] = jnp.zeros(low.shape[1:], BF16)
        for o in offsets:
            put[o + SPAN] = low[which[o + SPAN]]
            back_copy(put, got, o, kind).start()
        got[SPAN] = low[which[SPAN]]

    for put, got, kind, out, hbm in (
        (put_v, ret_v, 1, out_v, dv_hbm),
        (put_k, ret_k, 0, out_k, dk_hbm),
    ):
        for o in offsets:
            back_copy(put, got, o, kind).wait()
        for i in range(per_owner):
            acc = jnp.zeros(out.shape[1:], F32)
            for g in range(WIDTH):
                acc = acc + jnp.where(picks[g] == i, got[g].astype(F32), 0.0)
            out[i] = acc.astype(BF16)
        pltpu.make_async_copy(out, hbm, out_sem.at[kind]).start()

    for c in shares:
        c.wait_send()
    for u in range(per_head):
        dq_own(u).wait()

    def finish(j, carry):
        dq_copy(per_head + j).wait()
        return carry

    lax.fori_loop(0, units - per_head, finish, 0)
    pltpu.make_async_copy(out_v, dv_hbm, out_sem.at[1]).wait()
    pltpu.make_async_copy(out_k, dk_hbm, out_sem.at[0]).wait()


def per_device(queries, image_keys, image_values, out_grad, tile_counts, block_reads):
    n_seq, n_head = lax.axis_size("seq"), lax.axis_size("head")
    rows, cols = queries.shape
    per_owner, slots, _ = image_keys.shape
    head_cols = cols // n_head
    units = cols // UNIT
    sizes = (n_seq, n_head, per_owner, slots, head_cols)
    smem = pl.BlockSpec(memory_space=pltpu.SMEM)
    anywhere = pl.BlockSpec(memory_space=pl.ANY)
    image = (slots, HDIM)
    span = READS * slots
    vmem = pltpu.VMEM
    dma = pltpu.SemaphoreType.DMA
    query_grad, key_grad, value_grad = pl.pallas_call(
        functools.partial(kernel, sizes),
        out_shape=(
            jax.ShapeDtypeStruct(queries.shape, BF16),
            jax.ShapeDtypeStruct(image_keys.shape, BF16),
            jax.ShapeDtypeStruct(image_values.shape, BF16),
        ),
        in_specs=[smem, smem, anywhere, anywhere, anywhere, anywhere],
        out_specs=[anywhere] * 3,
        scratch_shapes=[
            vmem((per_owner, *image), BF16),
            vmem((per_owner, *image), BF16),
            vmem((WIDTH, *image), BF16),
            vmem((WIDTH, *image), BF16),
            vmem((WIDTH, *image), BF16),
            vmem((WIDTH, *image), BF16),
            vmem((WIDTH, *image), BF16),
            vmem((WIDTH, *image), BF16),
            vmem((units, rows, UNIT), BF16),
            vmem((units, rows, UNIT), BF16),
            vmem((units, rows, UNIT), BF16),
            vmem((span, HDIM), BF16),
            vmem((HDIM, span), BF16),
            vmem((span, HDIM), BF16),
            vmem((span, UNIT), F32),
            vmem((span, UNIT), F32),
            vmem((span, UNIT), F32),
            vmem((span, UNIT), F32),
            vmem((span, UNIT), BF16),
            vmem((span, UNIT), BF16),
            vmem((8, UNIT), F32),
            vmem((span, HDIM), F32),
            vmem((span, HDIM), F32),
            vmem((READS + 1, *image), BF16),
            vmem((READS + 1, *image), BF16),
            vmem((per_owner, *image), BF16),
            vmem((per_owner, *image), BF16),
            dma((2,)),
            dma((units,)),
            dma((units,)),
            dma((units,)),
            dma((units,)),
            dma((2, WIDTH)),
            dma((2, WIDTH)),
            dma((2, WIDTH)),
            dma((2, WIDTH)),
            dma((units,)),
            dma((units,)),
            dma((2,)),
        ],
        compiler_params=pltpu.CompilerParams(
            collective_id=0, has_side_effects=True, vmem_limit_bytes=48 * 1024 * 1024
        ),
        name="cross_attention_backward",
    )(tile_counts, block_reads, queries, image_keys, image_values, out_grad)
    return query_grad, key_grad, value_grad


def solution(mesh):
    in_specs = (
        P(("seq", "head"), None),
        P("seq", None, "head"),
        P("seq", None, "head"),
        P(("seq", "head"), None),
        P(),
        P(),
    )
    out_specs = (P(("seq", "head"), None), P("seq", None, "head"), P("seq", None, "head"))
    return jax.shard_map(
        per_device, mesh=mesh, in_specs=in_specs, out_specs=out_specs, check_vma=False
    )
```

time: 229 us -> 66.4 us (0.29)
  matrix products: 82.3 us -> 0 us
  Pallas kernels: 0 us -> 56.5 us
  starting transfers between devices: 49.2 us -> 0 us
  local copies, waits for them, and re-layouts: 43.2 us -> 7.88 us
  other arithmetic: 28.4 us -> 0 us
  waiting for transfers between devices: 12.6 us -> 0 us
  between operations: 10.2 us -> 0.66 us
    dot_general x50 -> x0, matrix products: 82.3 us -> none  [the longest x8 18.4 us: one_head(): jnp.einsum('kts,tkd->skd', attention_low, grad_one, preferred_element_typ...]
    pallas_call x0 -> x1, Pallas kernels: none -> 56.5 us  [per_device(): pl.pallas_call(functools.partial(kernel, sizes), out_shape=(jax.ShapeDtyp...]
    ppermute x8 -> x0, starting transfers between devices: 38.2 us -> none  [passed_along(): return lax.ppermute(block, axis, route)]
    concatenate x4 -> x0, local copies, waits for them, and re-layouts: 15.2 us -> none  [the longest x1 8.89 us: per_device(): jnp.concatenate([returned[offset] for offset in range(-SPAN, SPAN + 1)],...]
    all_to_all x3 -> x0, waiting for transfers between devices: 12.3 us -> none  [the longest x1 8.54 us: per_device(): lax.all_to_all(queries, 'head', split_axis=1, concat_axis=0, tiled=True)]
    all_to_all x3 -> x0, starting transfers between devices: 11 us -> none  [the longest x1 4.01 us: per_device(): lax.all_to_all(queries, 'head', split_axis=1, concat_axis=0, tiled=True)]
    reduce_sum x27 -> x0, other arithmetic: 9.57 us -> none  [the longest x8 4.57 us: one_head(): attention = unnormed / jnp.sum(unnormed, axis=-1, keepdims=True)]
    another operation x9 -> x0, other arithmetic: 9.05 us -> none  [the longest x5 7.52 us: per_device(): jnp.stack([back_keys[start:start + capacity], back_values[start:start + c...]
  transfers between devices with their start and end apart: 11 -> 0, of which waited for: 3 -> 0; matrix products, arithmetic and copies ran while one was open for 19% -> 0% of each run, Pallas kernels for 0% -> 0%
where the time goes in v1:
time: 66.4 us; the launch traced here: 65.1 us
  Pallas kernels  56.5 us (85%)
  local copies, waits for them, and re-layouts  7.88 us (12%)
    pallas_call x1, Pallas kernels, per_device(): pl.pallas_call(functools.partial(kernel, sizes), out_shape=(jax.ShapeDtyp...  56.5 us
    unnamed x14, local copies, waits for them, and re-layouts  7.88 us

profile of v1, /device:TPU:1, one launch (start us, length us, event | category | flops | bytes accessed | tf_op | source)
XLA Modules:
  0.0 65.1 jit_solution(16113493186999606639)
XLA Ops:
  0.6 0.0 copy-start.4
  0.6 0.8 %copy.9.reads_ref = s32[128,2]{1,0:T(8,128)S(1)} copy(s32[128,2]{0,1:T(2,128)} %param.11) | data formatting | bytes 2048 | tf_op args[5]
  1.4 0.0 copy-done.4
  1.4 0.0 copy-start
  1.4 1.2 %copy-done = bf16[128,4096]{1,0:T(8,128)(2,1)S(1)} copy-done((bf16[128,4096]{1,0:T(8,128)(2,1)S(1)}, bf16[128,4096]{1,0:T(8,128)(2,1)}, u32[]{:S(2)}) %copy-start) | copy-done | bytes 1048600
  2.7 0.0 copy-start.1
  2.7 1.2 %copy-done.1 = bf16[128,4096]{1,0:T(8,128)(2,1)S(1)} copy-done((bf16[128,4096]{1,0:T(8,128)(2,1)S(1)}, bf16[128,4096]{1,0:T(8,128)(2,1)}, u32[]{:S(2)}) %copy-start.1) | copy-done | bytes 1048600
  3.9 0.0 copy-start.2
  3.9 1.0 %copy-done.2 = bf16[4,512,128]{2,1,0:T(8,128)(2,1)S(1)} copy-done((bf16[4,512,128]{2,1,0:T(8,128)(2,1)S(1)}, bf16[4,512,128]{2,1,0:T(8,128)(2,1)}, u32[]{:S(2)}) %copy-start.2) | copy-done | bytes 524312
  4.9 0.0 copy-start.3
  4.9 1.0 %copy-done.3 = bf16[4,512,128]{2,1,0:T(8,128)(2,1)S(1)} copy-done((bf16[4,512,128]{2,1,0:T(8,128)(2,1)S(1)}, bf16[4,512,128]{2,1,0:T(8,128)(2,1)}, u32[]{:S(2)}) %copy-start.3) | copy-done | bytes 524312
  6.0 56.5 %cross_attention_backward.1 = (bf16[128,4096]{1,0:T(8,128)(2,1)S(1)}, bf16[4,512,128]{2,1,0:T(8,128)(2,1)S(1)}, bf16[4,512,128]{2,1,0:T(8,128)(2,1)S(1)}) custom-call(s32[512]{0:T(512)S(1)} %copy-done.4, s32[128,2]{1,0:T(8,128)S(1)} %copy.9.reads_ref, bf16[128,4096]{1,0:T(8,128)(2,1)S(1)} %copy-done, bf16[4,512,128]{2,1,0:T(8,128)(2,1)S(1)} %copy-done.2, ...), custom_call_target="tpu_custom_call" | custom-call | tf_op jit(solution)/shard_map/cross_attention_backward/pallas_call | solution.py:394
  62.5 1.0 %copy.13 = bf16[128,4096]{1,0:T(8,128)(2,1)} copy(bf16[128,4096]{1,0:T(8,128)(2,1)S(1)} %get-tuple-element.6) | data formatting | bytes 2097152
  63.5 0.8 %copy.14 = bf16[4,512,128]{2,1,0:T(8,128)(2,1)} copy(bf16[4,512,128]{2,1,0:T(8,128)(2,1)S(1)} %get-tuple-element.7) | data formatting | bytes 1048576
  64.3 0.8 %copy.15 = bf16[4,512,128]{2,1,0:T(8,128)(2,1)} copy(bf16[4,512,128]{2,1,0:T(8,128)(2,1)S(1)} %get-tuple-element.8) | data formatting | bytes 1048576
Async XLA Ops:
  0.6 0.8 %copy-start.4 = (s32[512]{0:T(512)S(1)}, s32[512]{0:T(512)}, u32[]{:S(2)}) copy-start(s32[512]{0:T(512)} %counts_ref.1) | copy-start | bytes 6148
  1.4 1.2 %copy-start = (bf16[128,4096]{1,0:T(8,128)(2,1)S(1)}, bf16[128,4096]{1,0:T(8,128)(2,1)}, u32[]{:S(2)}) copy-start(bf16[128,4096]{1,0:T(8,128)(2,1)} %q_hbm.1) | copy-start | bytes 3145732
  2.7 1.2 %copy-start.1 = (bf16[128,4096]{1,0:T(8,128)(2,1)S(1)}, bf16[128,4096]{1,0:T(8,128)(2,1)}, u32[]{:S(2)}) copy-start(bf16[128,4096]{1,0:T(8,128)(2,1)} %g_hbm.1) | copy-start | bytes 3145732
  3.9 1.0 %copy-start.2 = (bf16[4,512,128]{2,1,0:T(8,128)(2,1)S(1)}, bf16[4,512,128]{2,1,0:T(8,128)(2,1)}, u32[]{:S(2)}) copy-start(bf16[4,512,128]{2,1,0:T(8,128)(2,1)} %k_hbm.1) | copy-start | bytes 1572868
  4.9 1.0 %copy-start.3 = (bf16[4,512,128]{2,1,0:T(8,128)(2,1)S(1)}, bf16[4,512,128]{2,1,0:T(8,128)(2,1)}, u32[]{:S(2)}) copy-start(bf16[4,512,128]{2,1,0:T(8,128)(2,1)} %v_hbm.1) | copy-start | bytes 1572868

commit v2 on v1

--- a/solution.py
+++ b/solution.py
@@ -16,6 +16,7 @@
 SCALE2 = SCALE * 1.4426950408889634
 UNIT = 256
 PAIRS = UNIT // HDIM
+VMEM_LIMIT = 58 * 1024 * 1024
 F32 = jnp.float32
 BF16 = jnp.bfloat16
 MESH = pl.DeviceIdType.MESH
@@ -34,15 +35,17 @@
 
 def kernel(
     sizes,
-    counts_ref,
-    reads_ref,
+    counts_hbm,
+    reads_hbm,
     q_hbm,
     k_hbm,
     v_hbm,
     g_hbm,
     dq_hbm,
-    dk_hbm,
-    dv_hbm,
+    out_k,
+    out_v,
+    counts_ref,
+    reads_ref,
     own_k,
     own_v,
     put_k,
@@ -68,8 +71,6 @@
     sum_v,
     low_k,
     low_v,
-    out_k,
-    out_v,
     own_sem,
     q_sem,
     g_sem,
@@ -81,7 +82,6 @@
     back_recv,
     dq_send,
     dq_recv,
-    out_sem,
 ):
     n_seq, n_head, per_owner, slots, head_cols = sizes
     per_head = head_cols // UNIT
@@ -97,6 +97,10 @@
     def along_seq(o):
         return lax.rem(s + o + n_seq, n_seq)
 
+    load_reads = pltpu.make_async_copy(reads_hbm, reads_ref, own_sem.at[2])
+    load_counts = pltpu.make_async_copy(counts_hbm, counts_ref, own_sem.at[3])
+    load_reads.start()
+    load_counts.start()
     load_k = pltpu.make_async_copy(k_hbm, own_k, own_sem.at[0])
     load_v = pltpu.make_async_copy(v_hbm, own_v, own_sem.at[1])
     load_k.start()
@@ -121,11 +125,14 @@
         pl.semaphore_signal(barrier, inc=1, device_id=(along_seq(o), x), device_id_type=MESH)
     pl.semaphore_wait(barrier, n_head - 1 + len(offsets))
 
+    load_reads.wait()
+    load_counts.wait()
+
     picks = []
     for o in range(-SPAN, SPAN + 1):
         reader = along_seq(o)
-        first = reads_ref[reader, 0] - s * per_owner
-        second = reads_ref[reader, 1] - s * per_owner
+        first = reads_ref[0, reader] - s * per_owner
+        second = reads_ref[1, reader] - s * per_owner
         one = (first >= 0) & (first < per_owner)
         two = (second >= 0) & (second < per_owner)
         picks.append(jnp.where(one, first, jnp.where(two, second, 0)))
@@ -184,7 +191,7 @@
                 device_id_type=MESH,
             ).wait_recv()
 
-    images = [reads_ref[s, j] for j in range(READS)]
+    images = [reads_ref[j, s] for j in range(READS)]
     groups = [
         jnp.minimum(lax.rem(s - (images[j] // per_owner) + SPAN + n_seq, n_seq), WIDTH - 1)
         for j in range(READS)
@@ -351,9 +358,9 @@
             back_copy(put, got, o, kind).start()
         got[SPAN] = low[which[SPAN]]
 
-    for put, got, kind, out, hbm in (
-        (put_v, ret_v, 1, out_v, dv_hbm),
-        (put_k, ret_k, 0, out_k, dk_hbm),
+    for put, got, kind, out in (
+        (put_v, ret_v, 1, out_v),
+        (put_k, ret_k, 0, out_k),
     ):
         for o in offsets:
             back_copy(put, got, o, kind).wait()
@@ -362,7 +369,6 @@
             for g in range(WIDTH):
                 acc = acc + jnp.where(picks[g] == i, got[g].astype(F32), 0.0)
             out[i] = acc.astype(BF16)
-        pltpu.make_async_copy(out, hbm, out_sem.at[kind]).start()
 
     for c in shares:
         c.wait_send()
@@ -374,8 +380,18 @@
         return carry
 
     lax.fori_loop(0, units - per_head, finish, 0)
-    pltpu.make_async_copy(out_v, dv_hbm, out_sem.at[1]).wait()
-    pltpu.make_async_copy(out_k, dk_hbm, out_sem.at[0]).wait()
+
+
+def write_out(*refs):
+    sem = refs[-1]
+    half = (len(refs) - 1) // 2
+    copies = [
+        pltpu.make_async_copy(refs[i], refs[half + i], sem.at[i]) for i in range(half)
+    ]
+    for c in copies:
+        c.start()
+    for c in copies:
+        c.wait()
 
 
 def per_device(queries, image_keys, image_values, out_grad, tile_counts, block_reads):
@@ -385,22 +401,25 @@
     head_cols = cols // n_head
     units = cols // UNIT
     sizes = (n_seq, n_head, per_owner, slots, head_cols)
-    smem = pl.BlockSpec(memory_space=pltpu.SMEM)
+    inside = pl.BlockSpec(memory_space=pltpu.VMEM)
     anywhere = pl.BlockSpec(memory_space=pl.ANY)
     image = (slots, HDIM)
     span = READS * slots
     vmem = pltpu.VMEM
     dma = pltpu.SemaphoreType.DMA
-    query_grad, key_grad, value_grad = pl.pallas_call(
+    operands = (tile_counts, block_reads.T, queries, image_keys, image_values, out_grad)
+    grads = pl.pallas_call(
         functools.partial(kernel, sizes),
         out_shape=(
-            jax.ShapeDtypeStruct(queries.shape, BF16),
-            jax.ShapeDtypeStruct(image_keys.shape, BF16),
-            jax.ShapeDtypeStruct(image_values.shape, BF16),
+            pltpu.VMEM(queries.shape, BF16),
+            pltpu.VMEM(image_keys.shape, BF16),
+            pltpu.VMEM(image_values.shape, BF16),
         ),
-        in_specs=[smem, smem, anywhere, anywhere, anywhere, anywhere],
-        out_specs=[anywhere] * 3,
+        in_specs=[anywhere, anywhere, anywhere, anywhere, anywhere, anywhere],
+        out_specs=[inside] * 3,
         scratch_shapes=[
+            pltpu.SMEM(tile_counts.shape, jnp.int32),
+            pltpu.SMEM(block_reads.shape[::-1], jnp.int32),
             vmem((per_owner, *image), BF16),
             vmem((per_owner, *image), BF16),
             vmem((WIDTH, *image), BF16),
@@ -426,9 +445,7 @@
             vmem((span, HDIM), F32),
             vmem((READS + 1, *image), BF16),
             vmem((READS + 1, *image), BF16),
-            vmem((per_owner, *image), BF16),
-            vmem((per_owner, *image), BF16),
-            dma((2,)),
+            dma((4,)),
             dma((units,)),
             dma((units,)),
             dma((units,)),
@@ -439,14 +456,20 @@
             dma((2, WIDTH)),
             dma((units,)),
             dma((units,)),
-            dma((2,)),
         ],
         compiler_params=pltpu.CompilerParams(
-            collective_id=0, has_side_effects=True, vmem_limit_bytes=48 * 1024 * 1024
+            collective_id=0, has_side_effects=True, vmem_limit_bytes=VMEM_LIMIT
         ),
         name="cross_attention_backward",
-    )(tile_counts, block_reads, queries, image_keys, image_values, out_grad)
-    return query_grad, key_grad, value_grad
+    )(*(pltpu.with_memory_space_constraint(a, pltpu.HBM) for a in operands))
+    return pl.pallas_call(
+        write_out,
+        out_shape=[jax.ShapeDtypeStruct(a.shape, a.dtype) for a in grads],
+        in_specs=[inside] * 3,
+        out_specs=[anywhere] * 3,
+        scratch_shapes=[dma((3,))],
+        name="write_out",
+    )(*(pltpu.with_memory_space_constraint(a, pltpu.VMEM) for a in grads))
 
 
 def solution(mesh):

time: 66.4 us -> 57.8 us (0.87)
  local copies, waits for them, and re-layouts: 7.88 us -> 0 us
    unnamed x14 -> x0, local copies, waits for them, and re-layouts: 7.88 us -> none
    pallas_call x1 -> x2, Pallas kernels: 56.5 us -> 56.5 us  [the longest x1 55.1 us: per_device(): pl.pallas_call(functools.partial(kernel, sizes), out_shape=(pltpu.VMEM(qu...]
where the time goes in v2:
time: 57.8 us; the launch traced here: 57.1 us
  Pallas kernels  56.5 us (98%)
  between operations  0.64 us (1%)
    pallas_call x1, Pallas kernels, per_device(): pl.pallas_call(functools.partial(kernel, sizes), out_shape=(pltpu.VMEM(qu...  55.1 us
    pallas_call x1, Pallas kernels, per_device(): pl.pallas_call(write_out, out_shape=[jax.ShapeDtypeStruct(a.shape, a.dtyp...  1.34 us

profile of v2, /device:TPU:1, one launch (start us, length us, event | category | flops | bytes accessed | tf_op | source)
XLA Modules:
  0.0 57.1 jit_solution(13481683880943312863)
XLA Ops:
  0.6 55.1 %cross_attention_backward.1 = (bf16[128,4096]{1,0:T(8,128)(2,1)S(1)}, bf16[4,512,128]{2,1,0:T(8,128)(2,1)S(1)}, bf16[4,512,128]{2,1,0:T(8,128)(2,1)S(1)}) custom-call(s32[512]{0:T(512)} %counts_hbm.1, s32[2,128]{1,0:T(2,128)} %bitcast.1, bf16[128,4096]{1,0:T(8,128)(2,1)} %q_hbm.1, bf16[4,512,128]{2,1,0:T(8,128)(2,1)} %k_hbm.1, bf16[4,512,128]{2,1,0:T(8,128)(2,1)} %v_hbm.1, ...), custom_call_target="tpu_custom_call" | custom-call | tf_op jit(solution)/shard_map/cross_attention_backward/pallas_call | solution.py:411
  55.8 1.3 %write_out.1 = (bf16[128,4096]{1,0:T(8,128)(2,1)}, bf16[4,512,128]{2,1,0:T(8,128)(2,1)}, bf16[4,512,128]{2,1,0:T(8,128)(2,1)}) custom-call(bf16[128,4096]{1,0:T(8,128)(2,1)S(1)} %get-tuple-element.6.refs_0_, bf16[4,512,128]{2,1,0:T(8,128)(2,1)S(1)} %get-tuple-element.7.refs_1_, bf16[4,512,128]{2,1,0:T(8,128)(2,1)S(1)} %get-tuple-element.8.refs_2_), custom_call_target="tpu_custom_call" | custom-call | tf_op jit(solution)/shard_map/write_out/pallas_call | solution.py:465

commit v3 on v2

--- a/solution.py
+++ b/solution.py
@@ -66,6 +66,10 @@
     d1,
     att,
     dsc,
+    att_late,
+    dsc_late,
+    q_rows,
+    g_rows,
     row_max,
     sum_k,
     sum_v,
@@ -125,40 +129,6 @@
         pl.semaphore_signal(barrier, inc=1, device_id=(along_seq(o), x), device_id_type=MESH)
     pl.semaphore_wait(barrier, n_head - 1 + len(offsets))
 
-    load_reads.wait()
-    load_counts.wait()
-
-    picks = []
-    for o in range(-SPAN, SPAN + 1):
-        reader = along_seq(o)
-        first = reads_ref[0, reader] - s * per_owner
-        second = reads_ref[1, reader] - s * per_owner
-        one = (first >= 0) & (first < per_owner)
-        two = (second >= 0) & (second < per_owner)
-        picks.append(jnp.where(one, first, jnp.where(two, second, 0)))
-
-    def kv_copy(put, got, o, kind):
-        g = o + SPAN
-        return pltpu.make_async_remote_copy(
-            src_ref=put.at[g],
-            dst_ref=got.at[g],
-            send_sem=kv_send.at[kind, g],
-            recv_sem=kv_recv.at[kind, g],
-            device_id=(along_seq(o), x),
-            device_id_type=MESH,
-        )
-
-    load_k.wait()
-    for o in offsets:
-        put_k[o + SPAN] = own_k[picks[o + SPAN]]
-        kv_copy(put_k, got_k, o, 0).start()
-    got_k[SPAN] = own_k[picks[SPAN]]
-    load_v.wait()
-    for o in offsets:
-        put_v[o + SPAN] = own_v[picks[o + SPAN]]
-        kv_copy(put_v, got_v, o, 1).start()
-    got_v[SPAN] = own_v[picks[SPAN]]
-
     def share_copy(i, k, src, dst, ssem, rsem):
         u = per_head + (n_head - 1) * i + HOPS.index(k)
         to = along_head(k)
@@ -179,6 +149,40 @@
             shares.append(share_copy(i, k, g_hbm, g_all, gs_sem, g_sem))
     for c in shares:
         c.start()
+
+    load_reads.wait()
+    load_counts.wait()
+
+    picks = []
+    for o in range(-SPAN, SPAN + 1):
+        reader = along_seq(o)
+        first = reads_ref[0, reader] - s * per_owner
+        second = reads_ref[1, reader] - s * per_owner
+        one = (first >= 0) & (first < per_owner)
+        two = (second >= 0) & (second < per_owner)
+        picks.append(jnp.where(one, first, jnp.where(two, second, 0)))
+
+    def kv_copy(put, got, o, kind):
+        g = o + SPAN
+        return pltpu.make_async_remote_copy(
+            src_ref=put.at[g],
+            dst_ref=got.at[g],
+            send_sem=kv_send.at[kind, g],
+            recv_sem=kv_recv.at[kind, g],
+            device_id=(along_seq(o), x),
+            device_id_type=MESH,
+        )
+
+    load_k.wait()
+    for o in offsets:
+        put_k[o + SPAN] = own_k[picks[o + SPAN]]
+        kv_copy(put_k, got_k, o, 0).start()
+    got_k[SPAN] = own_k[picks[SPAN]]
+    load_v.wait()
+    for o in offsets:
+        put_v[o + SPAN] = own_v[picks[o + SPAN]]
+        kv_copy(put_v, got_v, o, 1).start()
+    got_v[SPAN] = own_v[picks[SPAN]]
 
     def await_share(u):
         for buf, ssem, rsem in ((q_all, qs_sem, q_sem), (g_all, gs_sem, g_sem)):
@@ -215,6 +219,7 @@
     def usable(i):
         return (i % tiles) < limits[i // tiles]
 
+    half_slots = slots // 2
     chunk = 512
     n_chunks = READS * slots // chunk
     chunk_tiles = chunk // TILE
@@ -271,18 +276,34 @@
         inverse = 1.0 / jnp.sum(total, axis=0, keepdims=True)
         row_dot = jnp.sum(weighted, axis=0, keepdims=True) * inverse
         q, g = heads_to_rows(q_all[u]), heads_to_rows(g_all[u])
+        cols = pl.ds(pl.multiple_of(u * UNIT, UNIT), UNIT)
+        q_rows[cols, :] = q
+        g_rows[cols, :] = g
         dq = None
-        for c in range(n_chunks):
-            for t in range(chunk_tiles):
-                rows = pl.ds((c * chunk_tiles + t) * TILE, TILE)
-                a = s_ref[rows, :] * inverse
-                att[rows, :] = a.astype(BF16)
-                dsc[rows, :] = (a * (d_ref[rows, :] - row_dot)).astype(BF16)
-            rows = pl.ds(c * chunk, chunk)
-            sum_v[rows, :] += dot(att[rows, :], g, NN)
-            sum_k[rows, :] += dot(dsc[rows, :], q, NN)
-            part = dot(keys_t[:, c * chunk : (c + 1) * chunk], dsc[rows, :], NN)
-            dq = part if dq is None else dq + part
+        for late in (False, True):
+            for j in range(READS):
+                start = j * slots + (half_slots if late else 0)
+                for t in range(half_slots // TILE):
+                    rows = pl.ds(start + t * TILE, TILE)
+                    a = s_ref[rows, :] * inverse
+                    low = a.astype(BF16)
+                    grad = (a * (d_ref[rows, :] - row_dot)).astype(BF16)
+                    if late:
+                        kept = pl.ds(j * half_slots + t * TILE, TILE)
+                        att_late[kept, cols] = low
+                        dsc_late[kept, cols] = grad
+                    else:
+                        att[rows, :] = low
+                        dsc[rows, :] = grad
+                rows = pl.ds(start, half_slots)
+                if late:
+                    grad = dsc_late[pl.ds(j * half_slots, half_slots), cols]
+                else:
+                    grad = dsc[rows, :]
+                    sum_v[rows, :] += dot(att[rows, :], g, NN)
+                    sum_k[rows, :] += dot(grad, q, NN)
+                part = dot(keys_t[:, start : start + half_slots], grad, NN)
+                dq = part if dq is None else dq + part
         dq = (dq * SCALE).T.astype(BF16)
         for h in range(PAIRS):
             dq_all[u, :, h * HDIM : (h + 1) * HDIM] = dq[h * HDIM : (h + 1) * HDIM]
@@ -331,13 +352,14 @@
     step(units - 1, 1, False)
     dq_copy(units - 1).start()
 
-    def back_copy(put, got, o, kind):
+    def back_copy(put, got, o, kind, half):
         g = o + SPAN
+        rows = pl.ds(half * half_slots, half_slots)
         return pltpu.make_async_remote_copy(
-            src_ref=put.at[g],
-            dst_ref=got.at[g],
-            send_sem=back_send.at[kind, g],
-            recv_sem=back_recv.at[kind, g],
+            src_ref=put.at[g, rows],
+            dst_ref=got.at[g, rows],
+            send_sem=back_send.at[kind, half, g],
+            recv_sem=back_recv.at[kind, half, g],
             device_id=(along_seq(-o), x),
             device_id_type=MESH,
         )
@@ -345,30 +367,40 @@
     which = []
     for g in range(WIDTH):
         which.append(jnp.where(groups[0] == g, 0, jnp.where(groups[1] == g, 1, READS)))
-    for low, total, factor, put, got, kind in (
-        (low_v, sum_v, None, put_v, ret_v, 1),
-        (low_k, sum_k, SCALE, put_k, ret_k, 0),
-    ):
-        for j in range(READS):
-            block = total[j * slots : (j + 1) * slots, :]
-            low[j] = (block if factor is None else block * factor).astype(BF16)
-        low[READS] = jnp.zeros(low.shape[1:], BF16)
-        for o in offsets:
-            put[o + SPAN] = low[which[o + SPAN]]
-            back_copy(put, got, o, kind).start()
-        got[SPAN] = low[which[SPAN]]
-
-    for put, got, kind, out in (
-        (put_v, ret_v, 1, out_v),
-        (put_k, ret_k, 0, out_k),
-    ):
-        for o in offsets:
-            back_copy(put, got, o, kind).wait()
-        for i in range(per_owner):
-            acc = jnp.zeros(out.shape[1:], F32)
-            for g in range(WIDTH):
-                acc = acc + jnp.where(picks[g] == i, got[g].astype(F32), 0.0)
-            out[i] = acc.astype(BF16)
+
+    def give_back(half):
+        for low, total, factor, put, got, kind, late, rows_of in (
+            (low_v, sum_v, None, put_v, ret_v, 1, att_late, g_rows),
+            (low_k, sum_k, SCALE, put_k, ret_k, 0, dsc_late, q_rows),
+        ):
+            for j in range(READS):
+                if half:
+                    block = dot(late[j * half_slots : (j + 1) * half_slots, :], rows_of[...], NN)
+                else:
+                    block = total[j * slots : j * slots + half_slots, :]
+                low[half, j] = (block if factor is None else block * factor).astype(BF16)
+            low[half, READS] = jnp.zeros(low.shape[2:], BF16)
+            rows = pl.ds(half * half_slots, half_slots)
+            for o in offsets:
+                put[o + SPAN, rows] = low[half, which[o + SPAN]]
+                back_copy(put, got, o, kind, half).start()
+            got[SPAN, rows] = low[half, which[SPAN]]
+
+    def take_back(half):
+        rows = pl.ds(half * half_slots, half_slots)
+        for put, got, kind, out in ((put_v, ret_v, 1, out_v), (put_k, ret_k, 0, out_k)):
+            for o in offsets:
+                back_copy(put, got, o, kind, half).wait()
+            for i in range(per_owner):
+                acc = jnp.zeros((half_slots, HDIM), F32)
+                for g in range(WIDTH):
+                    acc = acc + jnp.where(picks[g] == i, got[g, rows].astype(F32), 0.0)
+                out[i, rows] = acc.astype(BF16)
+
+    give_back(0)
+    give_back(1)
+    take_back(0)
+    take_back(1)
 
     for c in shares:
         c.wait_send()
@@ -440,11 +472,15 @@
             vmem((span, UNIT), F32),
             vmem((span, UNIT), BF16),
             vmem((span, UNIT), BF16),
+            vmem((span // 2, units * UNIT), BF16),
+            vmem((span // 2, units * UNIT), BF16),
+            vmem((units * UNIT, HDIM), BF16),
+            vmem((units * UNIT, HDIM), BF16),
             vmem((8, UNIT), F32),
             vmem((span, HDIM), F32),
             vmem((span, HDIM), F32),
-            vmem((READS + 1, *image), BF16),
-            vmem((READS + 1, *image), BF16),
+            vmem((2, READS + 1, slots // 2, HDIM), BF16),
+            vmem((2, READS + 1, slots // 2, HDIM), BF16),
             dma((4,)),
             dma((units,)),
             dma((units,)),
@@ -452,8 +488,8 @@
             dma((units,)),
             dma((2, WIDTH)),
             dma((2, WIDTH)),
-            dma((2, WIDTH)),
-            dma((2, WIDTH)),
+            dma((2, 2, WIDTH)),
+            dma((2, 2, WIDTH)),
             dma((units,)),
             dma((units,)),
         ],

time: 57.8 us -> 55.7 us (0.964); the launches traced: 57.1 us -> 55.6 us
  Pallas kernels: 56.5 us -> 54.9 us
    pallas_call x1, Pallas kernels: 55.1 us -> 53.6 us  [per_device(): pl.pallas_call(functools.partial(kernel, sizes), out_shape=(pltpu.VMEM(qu...]
where the time goes in v3:
time: 55.7 us; the launch traced here: 55.6 us
  Pallas kernels  54.9 us (99%)
  between operations  0.64 us (1%)
    pallas_call x1, Pallas kernels, per_device(): pl.pallas_call(functools.partial(kernel, sizes), out_shape=(pltpu.VMEM(qu...  53.6 us
    pallas_call x1, Pallas kernels, per_device(): pl.pallas_call(write_out, out_shape=[jax.ShapeDtypeStruct(a.shape, a.dtyp...  1.34 us

profile of v3, /device:TPU:1, one launch (start us, length us, event | category | flops | bytes accessed | tf_op | source)
XLA Modules:
  0.0 55.6 jit_solution(3922748806185969279)
XLA Ops:
  0.6 53.6 %cross_attention_backward.1 = (bf16[128,4096]{1,0:T(8,128)(2,1)S(1)}, bf16[4,512,128]{2,1,0:T(8,128)(2,1)S(1)}, bf16[4,512,128]{2,1,0:T(8,128)(2,1)S(1)}) custom-call(s32[512]{0:T(512)} %counts_hbm.1, s32[2,128]{1,0:T(2,128)} %bitcast.1, bf16[128,4096]{1,0:T(8,128)(2,1)} %q_hbm.1, bf16[4,512,128]{2,1,0:T(8,128)(2,1)} %k_hbm.1, bf16[4,512,128]{2,1,0:T(8,128)(2,1)} %v_hbm.1, ...), custom_call_target="tpu_custom_call" | custom-call | tf_op jit(solution)/shard_map/cross_attention_backward/pallas_call | solution.py:443
  54.2 1.3 %write_out.1 = (bf16[128,4096]{1,0:T(8,128)(2,1)}, bf16[4,512,128]{2,1,0:T(8,128)(2,1)}, bf16[4,512,128]{2,1,0:T(8,128)(2,1)}) custom-call(bf16[128,4096]{1,0:T(8,128)(2,1)S(1)} %get-tuple-element.6.refs_0_, bf16[4,512,128]{2,1,0:T(8,128)(2,1)S(1)} %get-tuple-element.7.refs_1_, bf16[4,512,128]{2,1,0:T(8,128)(2,1)S(1)} %get-tuple-element.8.refs_2_), custom_call_target="tpu_custom_call" | custom-call | tf_op jit(solution)/shard_map/write_out/pallas_call | solution.py:501

commit v4 on v3

--- a/solution.py
+++ b/solution.py
@@ -101,6 +101,13 @@
     def along_seq(o):
         return lax.rem(s + o + n_seq, n_seq)
 
+    barrier = pltpu.get_barrier_semaphore()
+    offsets = [o for o in range(-SPAN, SPAN + 1) if o != 0]
+    for k in range(1, n_head):
+        pl.semaphore_signal(barrier, inc=1, device_id=(s, along_head(k)), device_id_type=MESH)
+    for o in offsets:
+        pl.semaphore_signal(barrier, inc=1, device_id=(along_seq(o), x), device_id_type=MESH)
+
     load_reads = pltpu.make_async_copy(reads_hbm, reads_ref, own_sem.at[2])
     load_counts = pltpu.make_async_copy(counts_hbm, counts_ref, own_sem.at[3])
     load_reads.start()
@@ -121,12 +128,6 @@
         for c in own_load(u):
             c.start()
 
-    barrier = pltpu.get_barrier_semaphore()
-    offsets = [o for o in range(-SPAN, SPAN + 1) if o != 0]
-    for k in range(1, n_head):
-        pl.semaphore_signal(barrier, inc=1, device_id=(s, along_head(k)), device_id_type=MESH)
-    for o in offsets:
-        pl.semaphore_signal(barrier, inc=1, device_id=(along_seq(o), x), device_id_type=MESH)
     pl.semaphore_wait(barrier, n_head - 1 + len(offsets))
 
     def share_copy(i, k, src, dst, ssem, rsem):
@@ -250,7 +251,7 @@
             tops += score_chunk(q, g, halves[0], c)
         row_max[0:1, :] = finish_max(tops)
 
-    def step(u, b, more):
+    def step(u, b, more, values_done=None):
         s_ref, d_ref = halves[b]
         top = row_max[b : b + 1, :]
         total = jnp.zeros((8, UNIT), F32)
@@ -279,6 +280,14 @@
         cols = pl.ds(pl.multiple_of(u * UNIT, UNIT), UNIT)
         q_rows[cols, :] = q
         g_rows[cols, :] = g
+        if values_done is not None:
+            for j in range(READS):
+                rows = pl.ds(j * slots, half_slots)
+                for t in range(half_slots // TILE):
+                    tile = pl.ds(j * slots + t * TILE, TILE)
+                    att[tile, :] = (s_ref[tile, :] * inverse).astype(BF16)
+                sum_v[rows, :] += dot(att[rows, :], g, NN)
+            values_done()
         dq = None
         for late in (False, True):
             for j in range(READS):
@@ -293,14 +302,16 @@
                         att_late[kept, cols] = low
                         dsc_late[kept, cols] = grad
                     else:
-                        att[rows, :] = low
+                        if values_done is None:
+                            att[rows, :] = low
                         dsc[rows, :] = grad
                 rows = pl.ds(start, half_slots)
                 if late:
                     grad = dsc_late[pl.ds(j * half_slots, half_slots), cols]
                 else:
                     grad = dsc[rows, :]
-                    sum_v[rows, :] += dot(att[rows, :], g, NN)
+                    if values_done is None:
+                        sum_v[rows, :] += dot(att[rows, :], g, NN)
                     sum_k[rows, :] += dot(grad, q, NN)
                 part = dot(keys_t[:, start : start + half_slots], grad, NN)
                 dq = part if dq is None else dq + part
@@ -327,30 +338,29 @@
             device_id_type=MESH,
         )
 
-    first_scores()
-    for u in range(per_head - 1):
-        step(u, u % 2, True)
-        dq_own(u).start()
-    await_share(per_head)
-    step(per_head - 1, (per_head - 1) % 2, True)
-    dq_own(per_head - 1).start()
+    def await_unit(u):
+        @pl.when(u >= per_head)
+        def _():
+            await_share(u)
+
+    def send_dq(u):
+        @pl.when(u < per_head)
+        def _():
+            dq_own(u).start()
+
+        @pl.when(u >= per_head)
+        def _():
+            dq_copy(u).start()
 
     def two(j, carry):
-        u = per_head + 2 * j
-        await_share(u + 1)
+        u = 2 * j
+        await_unit(u + 1)
         step(u, 0, True)
-        dq_copy(u).start()
-        await_share(u + 2)
+        send_dq(u)
+        await_unit(u + 2)
         step(u + 1, 1, True)
-        dq_copy(u + 1).start()
+        send_dq(u + 1)
         return carry
-
-    lax.fori_loop(0, (units - per_head) // 2 - 1, two, 0)
-    await_share(units - 1)
-    step(units - 2, 0, True)
-    dq_copy(units - 2).start()
-    step(units - 1, 1, False)
-    dq_copy(units - 1).start()
 
     def back_copy(put, got, o, kind, half):
         g = o + SPAN
@@ -368,23 +378,23 @@
     for g in range(WIDTH):
         which.append(jnp.where(groups[0] == g, 0, jnp.where(groups[1] == g, 1, READS)))
 
-    def give_back(half):
-        for low, total, factor, put, got, kind, late, rows_of in (
-            (low_v, sum_v, None, put_v, ret_v, 1, att_late, g_rows),
-            (low_k, sum_k, SCALE, put_k, ret_k, 0, dsc_late, q_rows),
-        ):
-            for j in range(READS):
-                if half:
-                    block = dot(late[j * half_slots : (j + 1) * half_slots, :], rows_of[...], NN)
-                else:
-                    block = total[j * slots : j * slots + half_slots, :]
-                low[half, j] = (block if factor is None else block * factor).astype(BF16)
-            low[half, READS] = jnp.zeros(low.shape[2:], BF16)
-            rows = pl.ds(half * half_slots, half_slots)
-            for o in offsets:
-                put[o + SPAN, rows] = low[half, which[o + SPAN]]
-                back_copy(put, got, o, kind, half).start()
-            got[SPAN, rows] = low[half, which[SPAN]]
+    def give_back(half, kind):
+        low, total, factor, put, got, late, rows_of = (
+            (low_k, sum_k, SCALE, put_k, ret_k, dsc_late, q_rows),
+            (low_v, sum_v, None, put_v, ret_v, att_late, g_rows),
+        )[kind]
+        for j in range(READS):
+            if half:
+                block = dot(late[j * half_slots : (j + 1) * half_slots, :], rows_of[...], NN)
+            else:
+                block = total[j * slots : j * slots + half_slots, :]
+            low[half, j] = (block if factor is None else block * factor).astype(BF16)
+        low[half, READS] = jnp.zeros(low.shape[2:], BF16)
+        rows = pl.ds(half * half_slots, half_slots)
+        for o in offsets:
+            put[o + SPAN, rows] = low[half, which[o + SPAN]]
+            back_copy(put, got, o, kind, half).start()
+        got[SPAN, rows] = low[half, which[SPAN]]
 
     def take_back(half):
         rows = pl.ds(half * half_slots, half_slots)
@@ -397,29 +407,41 @@
                     acc = acc + jnp.where(picks[g] == i, got[g, rows].astype(F32), 0.0)
                 out[i, rows] = acc.astype(BF16)
 
-    give_back(0)
-    give_back(1)
-    take_back(0)
-    take_back(1)
-
+    first_scores()
+    lax.fori_loop(0, units // 2 - 1, two, 0)
+    await_share(units - 1)
+    step(units - 2, 0, True)
+    dq_copy(units - 2).start()
+    step(units - 1, 1, False, lambda: give_back(0, 1))
+    dq_copy(units - 1).start()
+    give_back(0, 0)
+    give_back(1, 1)
+    give_back(1, 0)
     for c in shares:
         c.wait_send()
     for u in range(per_head):
         dq_own(u).wait()
+    take_back(0)
 
     def finish(j, carry):
         dq_copy(per_head + j).wait()
         return carry
 
     lax.fori_loop(0, units - per_head, finish, 0)
+    take_back(1)
 
 
 def write_out(*refs):
     sem = refs[-1]
     half = (len(refs) - 1) // 2
-    copies = [
-        pltpu.make_async_copy(refs[i], refs[half + i], sem.at[i]) for i in range(half)
-    ]
+    copies = []
+    for i in range(half):
+        rows = refs[i].shape[0] // 4
+        for r in range(4):
+            part = pl.ds(r * rows, rows)
+            copies.append(
+                pltpu.make_async_copy(refs[i].at[part], refs[half + i].at[part], sem.at[i, r])
+            )
     for c in copies:
         c.start()
     for c in copies:
@@ -503,7 +525,7 @@
         out_shape=[jax.ShapeDtypeStruct(a.shape, a.dtype) for a in grads],
         in_specs=[inside] * 3,
         out_specs=[anywhere] * 3,
-        scratch_shapes=[dma((3,))],
+        scratch_shapes=[dma((3, 4))],
         name="write_out",
     )(*(pltpu.with_memory_space_constraint(a, pltpu.VMEM) for a in grads))
 

time: 55.7 us -> 55.7 us (level)
  no operation moved by 1% of the time
where the time goes in v4:
time: 55.7 us; the launch traced here: 55.6 us
  Pallas kernels  54.9 us (99%)
  between operations  0.64 us (1%)
    pallas_call x1, Pallas kernels, per_device(): pl.pallas_call(functools.partial(kernel, sizes), out_shape=(pltpu.VMEM(qu...  53.5 us
    pallas_call x1, Pallas kernels, per_device(): pl.pallas_call(write_out, out_shape=[jax.ShapeDtypeStruct(a.shape, a.dtyp...  1.41 us

profile of v4, /device:TPU:1, one launch (start us, length us, event | category | flops | bytes accessed | tf_op | source)
XLA Modules:
  0.0 55.6 jit_solution(15423870013941865562)
XLA Ops:
  0.6 53.5 %cross_attention_backward.1 = (bf16[128,4096]{1,0:T(8,128)(2,1)S(1)}, bf16[4,512,128]{2,1,0:T(8,128)(2,1)S(1)}, bf16[4,512,128]{2,1,0:T(8,128)(2,1)S(1)}) custom-call(s32[512]{0:T(512)} %counts_hbm.1, s32[2,128]{1,0:T(2,128)} %bitcast.1, bf16[128,4096]{1,0:T(8,128)(2,1)} %q_hbm.1, bf16[4,512,128]{2,1,0:T(8,128)(2,1)} %k_hbm.1, bf16[4,512,128]{2,1,0:T(8,128)(2,1)} %v_hbm.1, ...), custom_call_target="tpu_custom_call" | custom-call | tf_op jit(solution)/shard_map/cross_attention_backward/pallas_call | solution.py:465
  54.2 1.4 %write_out.1 = (bf16[128,4096]{1,0:T(8,128)(2,1)}, bf16[4,512,128]{2,1,0:T(8,128)(2,1)}, bf16[4,512,128]{2,1,0:T(8,128)(2,1)}) custom-call(bf16[128,4096]{1,0:T(8,128)(2,1)S(1)} %get-tuple-element.6.refs_0_, bf16[4,512,128]{2,1,0:T(8,128)(2,1)S(1)} %get-tuple-element.7.refs_1_, bf16[4,512,128]{2,1,0:T(8,128)(2,1)S(1)} %get-tuple-element.8.refs_2_), custom_call_target="tpu_custom_call" | custom-call | tf_op jit(solution)/shard_map/write_out/pallas_call | solution.py:523

commit v5 on v4

--- a/solution.py
+++ b/solution.py
@@ -102,7 +102,7 @@
         return lax.rem(s + o + n_seq, n_seq)
 
     barrier = pltpu.get_barrier_semaphore()
-    offsets = [o for o in range(-SPAN, SPAN + 1) if o != 0]
+    offsets = [o for d in range(SPAN, 0, -1) for o in (-d, d)]
     for k in range(1, n_head):
         pl.semaphore_signal(barrier, inc=1, device_id=(s, along_head(k)), device_id_type=MESH)
     for o in offsets:
@@ -221,7 +221,7 @@
         return (i % tiles) < limits[i // tiles]
 
     half_slots = slots // 2
-    chunk = 512
+    chunk = 1024
     n_chunks = READS * slots // chunk
     chunk_tiles = chunk // TILE
     halves = ((s0, d0), (s1, d1))

time: 55.7 us -> 55.6 us (level)
  no operation moved by 1% of the time
where the time goes in v5:
time: 55.6 us; the launch traced here: 55.4 us
  Pallas kernels  54.8 us (99%)
  between operations  0.64 us (1%)
    pallas_call x1, Pallas kernels, per_device(): pl.pallas_call(functools.partial(kernel, sizes), out_shape=(pltpu.VMEM(qu...  53.4 us
    pallas_call x1, Pallas kernels, per_device(): pl.pallas_call(write_out, out_shape=[jax.ShapeDtypeStruct(a.shape, a.dtyp...  1.41 us

profile of v5, /device:TPU:1, one launch (start us, length us, event | category | flops | bytes accessed | tf_op | source)
XLA Modules:
  0.0 55.4 jit_solution(13445875746003980928)
XLA Ops:
  0.6 53.4 %cross_attention_backward.1 = (bf16[128,4096]{1,0:T(8,128)(2,1)S(1)}, bf16[4,512,128]{2,1,0:T(8,128)(2,1)S(1)}, bf16[4,512,128]{2,1,0:T(8,128)(2,1)S(1)}) custom-call(s32[512]{0:T(512)} %counts_hbm.1, s32[2,128]{1,0:T(2,128)} %bitcast.1, bf16[128,4096]{1,0:T(8,128)(2,1)} %q_hbm.1, bf16[4,512,128]{2,1,0:T(8,128)(2,1)} %k_hbm.1, bf16[4,512,128]{2,1,0:T(8,128)(2,1)} %v_hbm.1, ...), custom_call_target="tpu_custom_call" | custom-call | tf_op jit(solution)/shard_map/cross_attention_backward/pallas_call | solution.py:465
  54.0 1.4 %write_out.1 = (bf16[128,4096]{1,0:T(8,128)(2,1)}, bf16[4,512,128]{2,1,0:T(8,128)(2,1)}, bf16[4,512,128]{2,1,0:T(8,128)(2,1)}) custom-call(bf16[128,4096]{1,0:T(8,128)(2,1)S(1)} %get-tuple-element.6.refs_0_, bf16[4,512,128]{2,1,0:T(8,128)(2,1)S(1)} %get-tuple-element.7.refs_1_, bf16[4,512,128]{2,1,0:T(8,128)(2,1)S(1)} %get-tuple-element.8.refs_2_), custom_call_target="tpu_custom_call" | custom-call | tf_op jit(solution)/shard_map/write_out/pallas_call | solution.py:523
